TPU v7x, 32 devices: a whole 2x2x4 slice. The times are simulated.
32 devices in a mesh: dp: 8 (over z, y), mp: 4 (over x, core).
Axes of the slice: x: 2, y: 2, z: 4, core: 2. Of those that a mesh axis runs over, the one named last changes fastest.
Arguments:
- tokens: bfloat16 [2, 8192, 768], P(None, 'dp'), may hold values from -6 to 6
- cotangent: bfloat16 [2, 8192, 768], P(None, 'dp'), may hold values from -6 to 6
- segments: int32 [8192], replicated, may hold values from 0 to 1, as said below
- route_query: int32 [2, 1024], P(None, 'dp'), may hold values from 0 to 1023, as said below
- route_key: int32 [2, 1024], replicated, may hold values from 0 to 1023, as said below
- route_ffn: int32 [2, 1024], P(None, 'dp'), may hold values from 0 to 1023, as said below
- attn_in: float32 [6, 768, 768], P(None, 'dp', 'mp'), may hold values from -0.21875 to 0.21875
- attn_out: float32 [2, 768, 768], P(None, ('mp', 'dp')), may hold values from -1.25 to 1.25
- light_in: float32 [2, 768, 1024], P(None, 'dp', 'mp'), may hold values from -0.21875 to 0.21875
- light_out: float32 [1024, 768], P(('mp', 'dp')), may hold values from -0.1875 to 0.1875
- heavy_in: float32 [2, 768, 4096], P(None, 'dp', 'mp'), may hold values from -0.21875 to 0.21875
- heavy_out: float32 [4096, 768], P(('mp', 'dp')), may hold values from -0.09375 to 0.09375
- gains: float32 [2, 768], P(None, 'dp'), may hold values from 0.4 to 3
- router: float32 [3, 768], P(None, 'dp'), may hold values from -0.21875 to 0.21875
- row_attn_in: float32 [6, 768], replicated, may hold values from 163.84 to 2621.44
- col_attn_in: float32 [6, 768], replicated, may hold values from 163.84 to 2621.44
- row_attn_out: float32 [2, 768], replicated, may hold values from 819.2 to 13107.2
- col_attn_out: float32 [2, 768], replicated, may hold values from 819.2 to 13107.2
- row_light_in: float32 [2, 768], replicated, may hold values from 819.2 to 13107.2
- col_light_in: float32 [2, 1024], replicated, may hold values from 819.2 to 13107.2
- row_light_out: float32 [1024], replicated, may hold values from 1638.4 to 26214.4
- col_light_out: float32 [768], replicated, may hold values from 1638.4 to 26214.4
- row_heavy_in: float32 [2, 768], replicated, may hold values from 81.92 to 1310.72
- col_heavy_in: float32 [2, 4096], replicated, may hold values from 81.92 to 1310.72
- row_heavy_out: float32 [4096], replicated, may hold values from 163.84 to 2621.44
- col_heavy_out: float32 [768], replicated, may hold values from 163.84 to 2621.44
- second_gains: float32 [2, 768], P(None, 'dp'), may hold values from 1638.4 to 26214.4
- second_router: float32 [3, 768], P(None, 'dp'), may hold values from 16384 to 262144
Outputs:
- mixed: bfloat16 [2, 8192, 768], P(None, 'dp')
- grad_tokens: float32 [2, 8192, 768], P(None, 'dp')
- grad_attn_in: float32 [6, 768, 768], P(None, 'dp', 'mp')
- rows_attn_in: float32 [6, 768], replicated
- cols_attn_in: float32 [6, 768], replicated
- new_attn_in: float32 [6, 768, 768], P(None, 'dp', 'mp')
- grad_attn_out: float32 [2, 768, 768], P(None, ('mp', 'dp'))
- rows_attn_out: float32 [2, 768], replicated
- cols_attn_out: float32 [2, 768], replicated
- new_attn_out: float32 [2, 768, 768], P(None, ('mp', 'dp'))
- grad_light_in: float32 [2, 768, 1024], P(None, 'dp', 'mp')
- rows_light_in: float32 [2, 768], replicated
- cols_light_in: float32 [2, 1024], replicated
- new_light_in: float32 [2, 768, 1024], P(None, 'dp', 'mp')
- grad_light_out: float32 [1024, 768], P(('mp', 'dp'))
- rows_light_out: float32 [1024], replicated
- cols_light_out: float32 [768], replicated
- new_light_out: float32 [1024, 768], P(('mp', 'dp'))
- grad_heavy_in: float32 [2, 768, 4096], P(None, 'dp', 'mp')
- rows_heavy_in: float32 [2, 768], replicated
- cols_heavy_in: float32 [2, 4096], replicated
- new_heavy_in: float32 [2, 768, 4096], P(None, 'dp', 'mp')
- grad_heavy_out: float32 [4096, 768], P(('mp', 'dp'))
- rows_heavy_out: float32 [4096], replicated
- cols_heavy_out: float32 [768], replicated
- new_heavy_out: float32 [4096, 768], P(('mp', 'dp'))
- grad_gains: float32 [2, 768], P(None, 'dp')
- moment_gains: float32 [2, 768], P(None, 'dp')
- new_gains: float32 [2, 768], P(None, 'dp')
- grad_router: float32 [3, 768], P(None, 'dp')
- moment_router: float32 [3, 768], P(None, 'dp')
- new_router: float32 [3, 768], P(None, 'dp')
Inputs may be any that keep to these rules, and one draw needn't show every extreme that they name: `segments`: ids never fall; every run of one id is 2048 tokens or longer. `route_query`: entries k * 128 to (k + 1) * 128 - 1 of a row are distinct rising token positions within the k-th block of 1024 tokens, counted from the block's start; in one block of each row the first and the last position are both among them. `route_key`: entries k * 128 to (k + 1) * 128 - 1 of a row are distinct rising token positions within the k-th block of 1024 tokens, counted from the block's start; in one block of each row the first and the last position are both among them. `route_ffn`: entries k * 128 to (k + 1) * 128 - 1 of a row are distinct rising token positions within the k-th block of 1024 tokens, counted from the block's start; in one block of each row the first and the last position are both among them.
All inputs are finite; a program needn't handle non-finite values.
Results may differ from a plain program's by a relative error of at most 0.024.
The roundings to bfloat16 on the way count: a program that leaves them out, or rounds other values in their place, can miss the bound.
Values may be sent and summed in bfloat16 or wider, within the bound.
No kernel may reach another device: no remote copies, remote signals or barrier semaphores. Data moves between devices by JAX's collectives and lax.ppermute only.
A program may use at most 256 MiB of HBM per device.

v0:
```python
import math

import jax
import jax.numpy as jnp
from jax import lax
from jax.sharding import PartitionSpec as P

D = 768
LH = 8
LDH = 96
HH = 12
HDH = 64
WIN = 128
STEP = 10


norm_eps = 1e-06
tiny_square = 1e-30
scale_floor = 0.001
clip_level = 1.0
step_rate = 0.5
masked_score = -1e30


def padded(cells, sides, width):
    for axis, dim in sides:
        count = lax.axis_size(axis)
        ends = count - 1
        head = lax.slice_in_dim(cells, 0, width, axis=dim)
        tail = lax.slice_in_dim(cells, cells.shape[dim] - width, cells.shape[dim], axis=dim)
        cells = jnp.concatenate(
            [
                lax.ppermute(tail, axis, [(i, (i + 1) % count) for i in range(ends)]),
                cells,
                lax.ppermute(head, axis, [((i + 1) % count, i) for i in range(ends)]),
            ],
            axis=dim,
        )
    return cells


def rms_norm(values, gain_row):
    return (
        values * lax.rsqrt(jnp.mean(values * values, axis=-1, keepdims=True) + norm_eps) * gain_row
    )


def norm_back(values, gain_row, upstream):
    normed_out, pullback = jax.vjp(rms_norm, values, gain_row)
    return pullback(upstream)


def gating_back(gate_up, upstream):

    def gating(gate_in, up_in):
        return jax.nn.gelu(gate_in) * up_in

    product, pullback = jax.vjp(gating, gate_up[0], gate_up[1])
    grad_gate, grad_up = pullback(upstream)
    return jnp.stack([grad_gate, grad_up]).astype(jnp.bfloat16)


def attend_fore(query_heads, key_heads, value_heads, allowed, scale_div):
    scores = (
        jnp.einsum("qhd,khd->hqk", query_heads, key_heads, preferred_element_type=jnp.float32)
        / scale_div
    )
    masked = jnp.where(allowed[None], scores, masked_score)
    top_score = jnp.max(masked, axis=-1, keepdims=True)
    exp_scores = jnp.exp(masked - top_score)
    exp_total = jnp.sum(exp_scores, axis=-1, keepdims=True)
    probs_low = (exp_scores / exp_total).astype(jnp.bfloat16)
    mixture = jnp.einsum("hqk,khd->qhd", probs_low, value_heads, preferred_element_type=jnp.float32)
    return (
        mixture.reshape(mixture.shape[0], -1).astype(jnp.bfloat16),
        top_score + jnp.log(exp_total),
    )


def attend_back(
    query_heads, key_heads, value_heads, allowed, log_total, grad_mix, scale_div, row_total
):
    scores = (
        jnp.einsum("qhd,khd->hqk", query_heads, key_heads, preferred_element_type=jnp.float32)
        / scale_div
    )
    soft_weights = jnp.exp(jnp.where(allowed[None], scores, masked_score) - log_total)
    soft_low = soft_weights.astype(jnp.bfloat16)
    grad_heads = grad_mix.reshape(query_heads.shape)
    grad_soft = jnp.einsum(
        "qhd,khd->hqk", grad_heads, value_heads, preferred_element_type=jnp.float32
    )
    grad_values = jnp.einsum(
        "hqk,qhd->khd", soft_low, grad_heads, preferred_element_type=jnp.float32
    )
    row_total = jnp.sum(soft_weights * grad_soft, axis=-1, keepdims=True)
    grad_scores = (soft_weights * (grad_soft - row_total)).astype(jnp.bfloat16)
    grad_query = (
        jnp.einsum("hqk,khd->qhd", grad_scores, key_heads, preferred_element_type=jnp.float32)
        / scale_div
    )
    grad_keys = (
        jnp.einsum("hqk,qhd->khd", grad_scores, query_heads, preferred_element_type=jnp.float32)
        / scale_div
    )
    query_count = query_heads.shape[0]
    key_count = key_heads.shape[0]
    return (
        grad_query.reshape(query_count, -1),
        grad_keys.reshape(key_count, -1),
        grad_values.reshape(key_count, -1),
        row_total,
    )


def scaled_step(weight, update, weight_sum, update_sum, count_all, lead_shape):
    rms_weight = jnp.sqrt(weight_sum / count_all).reshape(lead_shape)
    rms_update = jnp.sqrt(update_sum / count_all).reshape(lead_shape)
    step_size = (
        step_rate * jnp.maximum(scale_floor, rms_weight) / jnp.maximum(1.0, rms_update / clip_level)
    )
    return weight - step_size * update


def shards(
    tokens,
    cotangent,
    segments,
    route_query,
    route_key,
    route_ffn,
    attn_in,
    attn_out,
    light_in,
    light_out,
    heavy_in,
    heavy_out,
    gains,
    router,
    row_attn_in,
    col_attn_in,
    row_attn_out,
    col_attn_out,
    row_light_in,
    col_light_in,
    row_light_out,
    col_light_out,
    row_heavy_in,
    col_heavy_in,
    row_heavy_out,
    col_heavy_out,
    second_gains,
    second_router,
):
    data_size = lax.axis_size("dp")
    model_size = lax.axis_size("mp")
    data_index = lax.axis_index("dp")
    model_index = lax.axis_index("mp")
    micro_count = tokens.shape[0]
    tok_local = tokens.shape[1]
    routed_local = route_query.shape[1]
    routed_all = route_key.shape[1]
    radius = WIN // 2
    light_heads = LH // model_size
    heavy_heads = HH // model_size
    light_div = math.sqrt(LDH)
    heavy_div = math.sqrt(HDH)
    params = (attn_in, attn_out, light_in, light_out, heavy_in, heavy_out, gains, router)
    gather_dims = (1, 1, 1, 0, 1, 0, 1, 1)
    half_attn_in = attn_in.astype(jnp.bfloat16)
    half_attn_out = attn_out.astype(jnp.bfloat16)
    half_light_in = light_in.astype(jnp.bfloat16)
    half_light_out = light_out.astype(jnp.bfloat16)
    half_heavy_in = heavy_in.astype(jnp.bfloat16)
    half_heavy_out = heavy_out.astype(jnp.bfloat16)
    half_gains = gains.astype(jnp.bfloat16)
    half_router = router.astype(jnp.bfloat16)
    totals = []
    for shard_part, gather_dim in zip(params, gather_dims):
        full_shape = list(shard_part.shape)
        full_shape[gather_dim] = full_shape[gather_dim] * data_size
        totals.append(jnp.zeros(tuple(full_shape), jnp.float32))
    nearby = (
        jnp.abs(
            jnp.arange(tok_local)[:, None] - jnp.arange(tok_local + 2 * radius)[None, :] + radius
        )
        <= radius
    )
    key_block = jnp.arange(routed_all) // routed_local * tok_local
    mixed_list = []
    grad_list = []
    for micro_index in range(micro_count):
        fore_weights = (
            lax.all_gather(half_attn_in, "dp", axis=1, tiled=True),
            lax.all_gather(half_attn_out, "dp", axis=1, tiled=True),
            lax.all_gather(half_light_in, "dp", axis=1, tiled=True),
            lax.all_gather(half_light_out, "dp", axis=0, tiled=True),
            lax.all_gather(half_heavy_in, "dp", axis=1, tiled=True),
            lax.all_gather(half_heavy_out, "dp", axis=0, tiled=True),
            lax.all_gather(half_gains, "dp", axis=1, tiled=True),
            lax.all_gather(half_router, "dp", axis=1, tiled=True),
        )
        (
            w_attn_in,
            w_attn_out,
            w_light_in,
            w_light_out,
            w_heavy_in,
            w_heavy_out,
            w_gains,
            w_router,
        ) = fore_weights
        gain_rows = w_gains.astype(jnp.float32)
        route_rows = w_router.astype(jnp.float32)
        segment_ids = segments * (micro_index % 2)
        seg_padded = jnp.pad(segment_ids, (radius, radius), constant_values=-1)
        seg_local = lax.dynamic_slice_in_dim(segment_ids, data_index * tok_local, tok_local)
        seg_extended = lax.dynamic_slice_in_dim(
            seg_padded, data_index * tok_local, tok_local + 2 * radius
        )
        light_allowed = nearby & (seg_local[:, None] == seg_extended[None, :])
        query_local = route_query[micro_index]
        ffn_local = route_ffn[micro_index]
        key_global = route_key[micro_index]
        key_local = lax.dynamic_slice_in_dim(key_global, data_index * routed_local, routed_local)
        query_seg = seg_local[query_local]
        key_seg_all = segment_ids[key_global + key_block]
        heavy_allowed = query_seg[:, None] == key_seg_all[None, :]
        inputs = tokens[micro_index].astype(jnp.float32)
        normed = rms_norm(inputs, gain_rows[0])
        normed_low = normed.astype(jnp.bfloat16)
        light_proj = jnp.einsum(
            "td,sdf->stf", normed_low, w_attn_in[:3], preferred_element_type=jnp.float32
        ).astype(jnp.bfloat16)
        light_width = light_proj.shape[-1]
        extended = padded(
            jnp.concatenate([light_proj[1], light_proj[2]], axis=-1), (("dp", 0),), radius
        )
        light_query = light_proj[0].reshape(tok_local, light_heads, LDH)
        light_keys = extended[:, :light_width].reshape(-1, light_heads, LDH)
        light_values = extended[:, light_width:].reshape(-1, light_heads, LDH)
        light_mix, light_lse = attend_fore(
            light_query, light_keys, light_values, light_allowed, light_div
        )
        query_score = jax.nn.sigmoid(jnp.sum(normed[query_local] * route_rows[0], axis=-1))
        key_score = jax.nn.sigmoid(jnp.sum(normed[key_local] * route_rows[1], axis=-1))
        query_rows = normed_low[query_local]
        key_rows = normed_low[key_local]
        heavy_query = jnp.dot(query_rows, w_attn_in[3], preferred_element_type=jnp.float32).astype(
            jnp.bfloat16
        )
        heavy_key = jnp.dot(key_rows, w_attn_in[4], preferred_element_type=jnp.float32).astype(
            jnp.bfloat16
        )
        raw_value = jnp.dot(key_rows, w_attn_in[5], preferred_element_type=jnp.float32)
        scaled_value = (raw_value * key_score[:, None]).astype(jnp.bfloat16)
        heavy_width = heavy_key.shape[-1]
        heavy_pack = lax.all_gather(
            jnp.concatenate([heavy_key, scaled_value], axis=-1), "dp", axis=0, tiled=True
        )
        query_heads = heavy_query.reshape(routed_local, heavy_heads, HDH)
        key_heads = heavy_pack[:, :heavy_width].reshape(routed_all, heavy_heads, HDH)
        value_heads = heavy_pack[:, heavy_width:].reshape(routed_all, heavy_heads, HDH)
        heavy_mix, heavy_lse = attend_fore(
            query_heads, key_heads, value_heads, heavy_allowed, heavy_div
        )
        heavy_proj = jnp.dot(heavy_mix, w_attn_out[1], preferred_element_type=jnp.float32)
        attn_part = (
            jnp.dot(light_mix, w_attn_out[0], preferred_element_type=jnp.float32)
            .at[query_local]
            .add(query_score[:, None] * heavy_proj)
        )
        middle = inputs + lax.psum(attn_part.astype(jnp.bfloat16), "mp").astype(jnp.float32)
        normed_two = rms_norm(middle, gain_rows[1])
        low_two = normed_two.astype(jnp.bfloat16)
        gate_up = jnp.einsum("td,sdf->stf", low_two, w_light_in, preferred_element_type=jnp.float32)
        hidden = (jax.nn.gelu(gate_up[0]) * gate_up[1]).astype(jnp.bfloat16)
        ffn_score = jax.nn.sigmoid(jnp.sum(normed_two[ffn_local] * route_rows[2], axis=-1))
        ffn_rows = low_two[ffn_local]
        heavy_gate_up = jnp.einsum(
            "rd,sdf->srf", ffn_rows, w_heavy_in, preferred_element_type=jnp.float32
        )
        heavy_hidden = (jax.nn.gelu(heavy_gate_up[0]) * heavy_gate_up[1]).astype(jnp.bfloat16)
        heavy_out_rows = jnp.dot(heavy_hidden, w_heavy_out, preferred_element_type=jnp.float32)
        ffn_part = (
            jnp.dot(hidden, w_light_out, preferred_element_type=jnp.float32)
            .at[ffn_local]
            .add(ffn_score[:, None] * heavy_out_rows)
        )
        result = middle + lax.psum(ffn_part.astype(jnp.bfloat16), "mp").astype(jnp.float32)
        mixed_list.append(result.astype(jnp.bfloat16))
        (
            back_attn_in,
            back_attn_out,
            back_light_in,
            back_light_out,
            back_heavy_in,
            back_heavy_out,
            back_gains,
            back_router,
        ) = fore_weights
        upstream_low = cotangent[micro_index]
        upstream = upstream_low.astype(jnp.float32)
        grad_hidden = jnp.dot(upstream_low, back_light_out.T, preferred_element_type=jnp.float32)
        grad_gate_up = gating_back(gate_up, grad_hidden)
        totals[3] = totals[3] + jnp.dot(hidden.T, upstream_low, preferred_element_type=jnp.float32)
        totals[2] = totals[2] + jnp.einsum(
            "td,stf->sdf", low_two, grad_gate_up, preferred_element_type=jnp.float32
        )
        grad_two = jnp.einsum(
            "stf,sdf->td", grad_gate_up, back_light_in, preferred_element_type=jnp.float32
        )
        upstream_rows = upstream[ffn_local]
        grad_heavy_rows = (ffn_score[:, None] * upstream_rows).astype(jnp.bfloat16)
        grad_ffn_score = jnp.sum(upstream_rows * heavy_out_rows, axis=-1)
        totals[5] = totals[5] + jnp.dot(
            heavy_hidden.T, grad_heavy_rows, preferred_element_type=jnp.float32
        )
        grad_heavy_hidden = jnp.dot(
            grad_heavy_rows, back_heavy_out.T, preferred_element_type=jnp.float32
        )
        grad_heavy_gate_up = gating_back(heavy_gate_up, grad_heavy_hidden)
        totals[4] = totals[4] + jnp.einsum(
            "rd,srf->sdf", ffn_rows, grad_heavy_gate_up, preferred_element_type=jnp.float32
        )
        grad_two = grad_two.at[ffn_local].add(
            jnp.einsum(
                "srf,sdf->rd", grad_heavy_gate_up, back_heavy_in, preferred_element_type=jnp.float32
            )
        )
        grad_two, grad_ffn_score = (
            lax.psum(grad_two.astype(jnp.bfloat16), "mp").astype(jnp.float32),
            lax.psum(grad_ffn_score.astype(jnp.bfloat16), "mp").astype(jnp.float32),
        )
        ffn_logit = grad_ffn_score * ffn_score * (1.0 - ffn_score)
        totals[7] = totals[7].at[2].add(jnp.sum(ffn_logit[:, None] * normed_two[ffn_local], axis=0))
        grad_two = grad_two.at[ffn_local].add(ffn_logit[:, None] * route_rows[2])
        grad_middle_norm, grad_gain_two = norm_back(middle, gain_rows[1], grad_two)
        totals[6] = totals[6].at[1].add(grad_gain_two)
        grad_middle = upstream + grad_middle_norm
        attn_grad_low = grad_middle.astype(jnp.bfloat16)
        attn_grad = attn_grad_low.astype(jnp.float32)
        totals[1] = (
            totals[1]
            .at[0]
            .add(jnp.dot(light_mix.T, attn_grad_low, preferred_element_type=jnp.float32))
        )
        grad_light_mix = jnp.dot(
            attn_grad_low, back_attn_out[0].T, preferred_element_type=jnp.float32
        ).astype(jnp.bfloat16)
        grad_light_query, grad_keys_ext, grad_values_ext, light_rows_unused = attend_back(
            light_query,
            light_keys,
            light_values,
            light_allowed,
            light_lse,
            grad_light_mix,
            light_div,
            None,
        )
        grad_pack = jnp.concatenate([grad_keys_ext, grad_values_ext], axis=-1)
        rim_in = padded(
            jnp.concatenate([grad_pack[:radius], grad_pack[-radius:]], axis=0).astype(jnp.bfloat16),
            (("dp", 0),),
            radius,
        ).astype(jnp.float32)
        grad_inner = grad_pack[radius : radius + tok_local]
        grad_inner = (
            grad_inner.at[:radius]
            .add(rim_in[:radius])
            .at[tok_local - radius :]
            .add(rim_in[3 * radius :])
        )
        grad_light = jnp.stack(
            [grad_light_query, grad_inner[:, :light_width], grad_inner[:, light_width:]]
        ).astype(jnp.bfloat16)
        totals[0] = (
            totals[0]
            .at[:3]
            .add(
                jnp.einsum(
                    "td,stf->sdf", normed_low, grad_light, preferred_element_type=jnp.float32
                )
            )
        )
        grad_one = jnp.einsum(
            "stf,sdf->td", grad_light, back_attn_in[:3], preferred_element_type=jnp.float32
        )
        grad_rows = attn_grad[query_local]
        grad_heavy_proj = (query_score[:, None] * grad_rows).astype(jnp.bfloat16)
        grad_query_score = jnp.sum(grad_rows * heavy_proj, axis=-1)
        totals[1] = (
            totals[1]
            .at[1]
            .add(jnp.dot(heavy_mix.T, grad_heavy_proj, preferred_element_type=jnp.float32))
        )
        grad_heavy_mix = jnp.dot(
            grad_heavy_proj, back_attn_out[1].T, preferred_element_type=jnp.float32
        ).astype(jnp.bfloat16)
        grad_heavy_query, grad_key_all, grad_value_all, heavy_row_total = attend_back(
            query_heads,
            key_heads,
            value_heads,
            heavy_allowed,
            heavy_lse,
            grad_heavy_mix,
            heavy_div,
            None,
        )
        heavy_term = jnp.concatenate([grad_key_all, grad_value_all], axis=-1)
        heavy_mine = lax.psum_scatter(heavy_term, "dp", scatter_dimension=0, tiled=True)
        grad_key_low = heavy_mine[:, :heavy_width].astype(jnp.bfloat16)
        grad_scaled = heavy_mine[:, heavy_width:].astype(jnp.bfloat16).astype(jnp.float32)
        grad_raw_low = (grad_scaled * key_score[:, None]).astype(jnp.bfloat16)
        grad_key_score = jnp.sum(grad_scaled * raw_value, axis=-1)
        grad_query_low = grad_heavy_query.astype(jnp.bfloat16)
        totals[0] = (
            totals[0]
            .at[3]
            .add(jnp.dot(query_rows.T, grad_query_low, preferred_element_type=jnp.float32))
        )
        totals[0] = (
            totals[0]
            .at[4]
            .add(jnp.dot(key_rows.T, grad_key_low, preferred_element_type=jnp.float32))
        )
        totals[0] = (
            totals[0]
            .at[5]
            .add(jnp.dot(key_rows.T, grad_raw_low, preferred_element_type=jnp.float32))
        )
        grad_one = grad_one.at[query_local].add(
            jnp.dot(grad_query_low, back_attn_in[3].T, preferred_element_type=jnp.float32)
        )
        grad_one = grad_one.at[key_local].add(
            jnp.dot(grad_key_low, back_attn_in[4].T, preferred_element_type=jnp.float32)
            + jnp.dot(grad_raw_low, back_attn_in[5].T, preferred_element_type=jnp.float32)
        )
        grad_one, grad_query_score, grad_key_score = (
            lax.psum(grad_one.astype(jnp.bfloat16), "mp").astype(jnp.float32),
            lax.psum(grad_query_score.astype(jnp.bfloat16), "mp").astype(jnp.float32),
            lax.psum(grad_key_score.astype(jnp.bfloat16), "mp").astype(jnp.float32),
        )
        query_logit = grad_query_score * query_score * (1.0 - query_score)
        key_logit = grad_key_score * key_score * (1.0 - key_score)
        totals[7] = totals[7].at[0].add(jnp.sum(query_logit[:, None] * normed[query_local], axis=0))
        totals[7] = totals[7].at[1].add(jnp.sum(key_logit[:, None] * normed[key_local], axis=0))
        grad_one = grad_one.at[query_local].add(query_logit[:, None] * route_rows[0])
        grad_one = grad_one.at[key_local].add(key_logit[:, None] * route_rows[1])
        grad_inputs_norm, grad_gain_one = norm_back(inputs, gain_rows[0], grad_one)
        totals[6] = totals[6].at[0].add(grad_gain_one)
        grad_list.append(grad_middle + grad_inputs_norm)
    mixed = jnp.stack(mixed_list)
    grad_tokens = jnp.stack(grad_list)
    reduced = (
        lax.psum_scatter(totals[0], "dp", scatter_dimension=1, tiled=True),
        lax.psum_scatter(totals[1], "dp", scatter_dimension=1, tiled=True),
        lax.psum_scatter(totals[2], "dp", scatter_dimension=1, tiled=True),
        lax.psum_scatter(totals[3], "dp", scatter_dimension=0, tiled=True),
        lax.psum_scatter(totals[4], "dp", scatter_dimension=1, tiled=True),
        lax.psum_scatter(totals[5], "dp", scatter_dimension=0, tiled=True),
        lax.psum_scatter(totals[6], "dp", scatter_dimension=1, tiled=True),
        lax.psum_scatter(totals[7], "dp", scatter_dimension=1, tiled=True),
    )
    lead_flag = (model_index == 0).astype(jnp.float32)
    local_spot = model_index * data_size + data_index
    specs = (
        (
            attn_in,
            reduced[0],
            row_attn_in,
            col_attn_in,
            data_index * attn_in.shape[-2],
            model_index * attn_in.shape[-1],
        ),
        (attn_out, reduced[1], row_attn_out, col_attn_out, local_spot * attn_out.shape[-2], 0),
        (
            light_in,
            reduced[2],
            row_light_in,
            col_light_in,
            data_index * light_in.shape[-2],
            model_index * light_in.shape[-1],
        ),
        (light_out, reduced[3], row_light_out, col_light_out, local_spot * light_out.shape[-2], 0),
        (
            heavy_in,
            reduced[4],
            row_heavy_in,
            col_heavy_in,
            data_index * heavy_in.shape[-2],
            model_index * heavy_in.shape[-1],
        ),
        (heavy_out, reduced[5], row_heavy_out, col_heavy_out, local_spot * heavy_out.shape[-2], 0),
    )
    vector_specs = ((gains, reduced[6], second_gains), (router, reduced[7], second_router))
    row_parts = []
    col_parts = []
    weight_parts = []
    for weight, gradient, row_old, col_old, row_start, col_start in specs:
        square = gradient * gradient + tiny_square
        row_parts.append(
            lax.dynamic_update_slice_in_dim(
                jnp.zeros(row_old.shape, jnp.float32),
                jnp.sum(square, axis=-1),
                row_start,
                row_old.ndim - 1,
            ).reshape(-1)
        )
        col_parts.append(
            lax.dynamic_update_slice_in_dim(
                jnp.zeros(col_old.shape, jnp.float32),
                jnp.sum(square, axis=-2),
                col_start,
                col_old.ndim - 1,
            ).reshape(-1)
        )
        weight_parts.append(jnp.sum(weight * weight, axis=(-2, -1)).reshape(-1))
    for weight, gradient, second_old in vector_specs:
        weight_parts.append(jnp.sum(weight * weight, axis=-1) * lead_flag)
    row_sums, col_sums, weight_sums = lax.psum(
        (jnp.concatenate(row_parts), jnp.concatenate(col_parts), jnp.concatenate(weight_parts)),
        ("dp", "mp"),
    )
    decay_rate = 1.0 - STEP ** (-0.8)
    row_at = 0
    col_at = 0
    sum_at = 0
    pending = []
    update_parts = []
    for weight, gradient, row_old, col_old, row_start, col_start in specs:
        row_sum = row_sums[row_at : row_at + row_old.size].reshape(row_old.shape)
        col_sum = col_sums[col_at : col_at + col_old.size].reshape(col_old.shape)
        lead_count = row_old.size // row_old.shape[-1]
        weight_sum = weight_sums[sum_at : sum_at + lead_count]
        row_at = row_at + row_old.size
        col_at = col_at + col_old.size
        sum_at = sum_at + lead_count
        row_new = decay_rate * row_old + (1.0 - decay_rate) * row_sum / col_old.shape[-1]
        col_new = decay_rate * col_old + (1.0 - decay_rate) * col_sum / row_old.shape[-1]
        row_mean = jnp.mean(row_new, axis=-1)[..., None, None]
        my_rows = lax.dynamic_slice_in_dim(row_new, row_start, weight.shape[-2], row_new.ndim - 1)
        my_cols = lax.dynamic_slice_in_dim(col_new, col_start, weight.shape[-1], col_new.ndim - 1)
        update = gradient * lax.rsqrt(my_rows[..., :, None] * my_cols[..., None, :] / row_mean)
        update_parts.append(jnp.sum(update * update, axis=(-2, -1)).reshape(-1))
        pending.append(
            (
                weight,
                gradient,
                update,
                row_new,
                col_new,
                weight_sum,
                row_old.shape[-1] * col_old.shape[-1],
                weight.shape[:-2] + (1, 1),
                lead_count,
            )
        )
    vector_pending = []
    for weight, gradient, second_old in vector_specs:
        lead_count = weight.shape[0]
        weight_sum = weight_sums[sum_at : sum_at + lead_count]
        sum_at = sum_at + lead_count
        second_new = decay_rate * second_old + (1.0 - decay_rate) * (
            gradient * gradient + tiny_square
        )
        update = gradient * lax.rsqrt(second_new)
        update_parts.append(jnp.sum(update * update, axis=-1) * lead_flag)
        vector_pending.append((weight, gradient, update, second_new, weight_sum, lead_count))
    update_sums = lax.psum(jnp.concatenate(update_parts), ("dp", "mp"))
    results = [mixed, grad_tokens]
    used_at = 0
    for (
        weight,
        gradient,
        update,
        row_new,
        col_new,
        weight_sum,
        count_all,
        lead_shape,
        lead_count,
    ) in pending:
        update_sum = update_sums[used_at : used_at + lead_count]
        used_at = used_at + lead_count
        new_weight = scaled_step(weight, update, weight_sum, update_sum, count_all, lead_shape)
        results.extend([gradient, row_new, col_new, new_weight])
    for weight, gradient, update, second_new, weight_sum, lead_count in vector_pending:
        update_sum = update_sums[used_at : used_at + lead_count]
        used_at = used_at + lead_count
        new_weight = scaled_step(weight, update, weight_sum, update_sum, D, (lead_count, 1))
        results.extend([gradient, second_new, new_weight])
    return tuple(results)


def solution(mesh):
    placed = (
        P(None, "dp", None),
        P(None, "dp", None),
        P(),
        P(None, "dp"),
        P(),
        P(None, "dp"),
        P(None, "dp", "mp"),
        P(None, ("mp", "dp"), None),
        P(None, "dp", "mp"),
        P(("mp", "dp"), None),
        P(None, "dp", "mp"),
        P(("mp", "dp"), None),
        P(None, "dp"),
        P(None, "dp"),
        P(),
        P(),
        P(),
        P(),
        P(),
        P(),
        P(),
        P(),
        P(),
        P(),
        P(),
        P(),
        P(None, "dp"),
        P(None, "dp"),
    )
    return jax.shard_map(
        shards,
        mesh=mesh,
        in_specs=placed,
        out_specs=(
            P(None, "dp", None),
            P(None, "dp", None),
            P(None, "dp", "mp"),
            P(),
            P(),
            P(None, "dp", "mp"),
            P(None, ("mp", "dp"), None),
            P(),
            P(),
            P(None, ("mp", "dp"), None),
            P(None, "dp", "mp"),
            P(),
            P(),
            P(None, "dp", "mp"),
            P(("mp", "dp"), None),
            P(),
            P(),
            P(("mp", "dp"), None),
            P(None, "dp", "mp"),
            P(),
            P(),
            P(None, "dp", "mp"),
            P(("mp", "dp"), None),
            P(),
            P(),
            P(("mp", "dp"), None),
            P(None, "dp"),
            P(None, "dp"),
            P(None, "dp"),
            P(None, "dp"),
            P(None, "dp"),
            P(None, "dp"),
        ),
        check_vma=False,
    )
```

profile of v0, /device:TPU:0, one launch (start us, length us, event | category | flops | bytes accessed | tf_op | source)
XLA Modules:
  0.0 1893.3 jit_solution(6858856794381276922)
XLA Ops:
  14.1 22.2 %all-gather = bf16[8,96,2]{1,2,0:T(2,128)(2,1)S(1)} all-gather(bf16[1,96,2]{1,2,0:T(2,128)(2,1)S(1)} %get-tuple-element.740), channel_id=1, replica_groups=mesh['dp'=8,'mp'=4] {'dp'}, dimensions={0}, use_global_device_ids=true | all-gather | bytes 3456 | tf_op jit(solution)/shard_map/all_gather | solution.py:200
  73.9 16.4 all-gather.1
  109.0 33.6 %all_gather.40 = bf16[2,192,768]{2,1,0:T(8,128)(2,1)} all-gather(bf16[2,24,768]{2,1,0:T(8,128)(2,1)S(1)} %get-tuple-element.721), channel_id=1, replica_groups=mesh['dp'=8,'mp'=4] {'dp'}, dimensions={1}, use_global_device_ids=true | all-gather | bytes 663552 | tf_op jit(solution)/shard_map/all_gather | solution.py:195
  182.6 27.7 %all_gather.42 = bf16[1024,384]{0,1:T(8,128)(2,1)S(1)} all-gather(bf16[128,384]{0,1:T(8,128)(2,1)S(1)} %pad_maximum_fusion.27), channel_id=1, replica_groups=mesh['dp'=8,'mp'=4] {'dp'}, dimensions={0}, use_global_device_ids=true | all-gather | bytes 884736 | tf_op jit(solution)/shard_map/all_gather | solution.py:258
  210.4 28.5 %all_gather.47 = bf16[1024,384]{0,1:T(8,128)(2,1)S(1)} all-gather(bf16[128,384]{0,1:T(8,128)(2,1)S(1)} %pad_maximum_fusion.28), channel_id=1, replica_groups=mesh['dp'=8,'mp'=4] {'dp'}, dimensions={0}, use_global_device_ids=true | all-gather | bytes 884736 | tf_op jit(solution)/shard_map/all_gather | solution.py:258
  320.2 31.3 %all_gather.44 = bf16[256,768]{1,0:T(8,128)(2,1)S(1)} all-gather(bf16[32,768]{1,0:T(8,128)(2,1)S(1)} %get-tuple-element.723), channel_id=1, replica_groups=mesh['dp'=8,'mp'=4] {'dp'}, dimensions={0}, use_global_device_ids=true | all-gather | bytes 442368 | tf_op jit(solution)/shard_map/all_gather | solution.py:197
  351.6 33.6 %all_gather.43 = bf16[2,768,256]{2,1,0:T(8,128)(2,1)} all-gather(bf16[2,96,256]{2,1,0:T(8,128)(2,1)S(1)} %get-tuple-element.719), channel_id=1, replica_groups=mesh['dp'=8,'mp'=4] {'dp'}, dimensions={1}, use_global_device_ids=true | all-gather | bytes 884736 | tf_op jit(solution)/shard_map/all_gather | solution.py:196
  447.2 39.2 %all-gather.10.cloned.1.call-done = bf16[1024,768]{1,0:T(8,128)(2,1)} async-done(((bf16[128,768]{1,0:T(8,128)(2,1)}), bf16[1024,768]{1,0:T(8,128)(2,1)}) %all-gather.10.cloned.1.call-update) | async-done | bytes 1572880 | tf_op jit(solution)/shard_map/all_gather | solution.py:199
  555.2 39.6 %all-reduce.25.cloned.1.call-done = (bf16[1024,768]{1,0:T(8,128)(2,1)}, bf16[1024,768]{1,0:T(8,128)(2,1)}) async-done(((bf16[1024,768]{1,0:T(8,128)(2,1)}, bf16[1024,768]{1,0:T(8,128)(2,1)}), (bf16[1024,768]{1,0:T(8,128)(2,1)}, bf16[1024,768]{1,0:T(8,128)(2,1)})) %all-reduce.25.cloned.1.call-update) | async-done | bytes 3145744 | tf_op jit(solution)/shard_map/psum | solution.py:332
  649.6 7.7 multiply_reduce_fusion
  763.2 35.7 %reduce-scatter.17.cloned.1.call-done = f32[128,384]{0,1:T(8,128)} async-done(((f32[1024,384]{0,1:T(8,128)}), f32[128,384]{0,1:T(8,128)}) %reduce-scatter.17.cloned.1.call-update) | async-done | bytes 196624 | tf_op jit(solution)/shard_map/reduce_scatter | solution.py:411
  880.0 10.7 copy.198
  910.2 28.1 %all-reduce.23.cloned.1.call-done = (bf16[1024,768]{1,0:T(8,128)(2,1)}, bf16[1024,768]{1,0:T(8,128)(2,1)}, bf16[1024,768]{1,0:T(8,128)(2,1)}, bf16[1024,768]{1,0:T(8,128)(2,1)}) async-done(((bf16[1024,768]{1,0:T(8,128)(2,1)}, bf16[1024,768]{1,0:T(8,128)(2,1)}, bf16[1024,768]{1,0:T(8,128)(2,1)}, bf16[1024,768]{1,0:T(8,128)(2,1)}), (bf16[1024,768]{1,0:T(8,128)(2,1)}, bf16[1024,768]{1,0:T(8,128)(2,1)}, ...) | async-done | bytes 6291472 | tf_op jit(solution)/shard_map/psum | solution.py:290
  991.4 14.0 reduce-scatter.21.cloned.1.call-done
  1007.1 65.6 %reduce-scatter.19.cloned.1.call-done = f32[2,24,768]{2,1,0:T(8,128)} async-done(((f32[2,192,768]{2,1,0:T(8,128)}), f32[2,24,768]{2,1,0:T(8,128)}) %reduce-scatter.19.cloned.1.call-update) | async-done | bytes 147472 | tf_op jit(solution)/shard_map/reduce_scatter | solution.py:457
  1074.5 62.8 %reduce-scatter.29.cloned.1.call-done = f32[96,3]{1,0:T(8,128)} async-done(((f32[768,3]{1,0:T(8,128)}), f32[96,3]{1,0:T(8,128)}) %reduce-scatter.29.cloned.1.call-update) | async-done | bytes 1168
  1139.4 75.9 %reduce-scatter.23.cloned.1.call-done = f32[128,768]{1,0:T(8,128)} async-done(((f32[1024,768]{1,0:T(8,128)}), f32[128,768]{1,0:T(8,128)}) %reduce-scatter.23.cloned.1.call-update) | async-done | bytes 393232 | tf_op jit(solution)/shard_map/reduce_scatter | solution.py:461
  1217.2 257.9 %all-reduce.21.cloned.1.call-done = (f32[2,768,256]{2,0,1:T(2,128)}, f32[2,768,1024]{2,0,1:T(2,128)}) async-done(((f32[2,768,256]{2,0,1:T(2,128)}, f32[2,768,1024]{2,0,1:T(2,128)}), (f32[2,768,256]{2,0,1:T(2,128)}, f32[2,768,1024]{2,0,1:T(2,128)})) %all-reduce.21.cloned.1.call-update) | async-done | bytes 7864336
  1483.0 7.7 fusion.20
  1495.8 43.8 %reduce-scatter.27.cloned.1.call-done = f32[96,2]{1,0:T(8,128)} async-done(((f32[768,2]{1,0:T(8,128)}), f32[96,2]{1,0:T(8,128)}) %reduce-scatter.27.cloned.1.call-update) | async-done | bytes 784
  1541.7 79.7 %reduce-scatter.25.cloned.1.call-done = f32[96,1152]{1,0:T(8,128)} async-done(((f32[768,1152]{1,0:T(8,128)}), f32[96,1152]{1,0:T(8,128)}) %reduce-scatter.25.cloned.1.call-update) | async-done | bytes 442384
  1630.9 41.1 %psum.140 = f32[14336]{0:T(1024)S(1)} all-reduce(f32[14336]{0:T(1024)} %constant_dynamic-update-slice_fusion.5), channel_id=1, replica_groups=mesh['dp'=8,'mp'=4] {'dp','mp'}, use_global_device_ids=true, to_apply=%region_76.77 | all-reduce | flops 14336 | bytes 114688 | tf_op jit(solution)/shard_map/psum | solution.py:521
  1700.8 101.5 %all-reduce.19.cloned.1.call-done = f32[17920]{0:T(1024)} async-done(((f32[17920]{0:T(1024)}), f32[17920]{0:T(1024)}) %all-reduce.19.cloned.1.call-update) | async-done | bytes 71696 | tf_op jit(solution)/shard_map/psum | solution.py:521
  1828.7 42.0 %all-reduce.6 = (f32[19]{0:T(128)S(1)}, f32[19]{0:T(128)S(1)}) all-reduce(f32[19]{0:T(128)S(1)} %concatenate.123, f32[19]{0:T(128)S(1)} %copy-done.284), channel_id=1, replica_groups=mesh['dp'=8,'mp'=4] {'dp','mp'}, use_global_device_ids=true, to_apply=%region_119.120 | all-reduce | flops 38 | bytes 304 | tf_op jit(solution)/shard_map/psum | solution.py:570
  (1064 shorter events, 724.4 us)
Async XLA Ops:
  7.2 140.3 %all-gather.6.cloned.1.call-start = ((), (), s32[]{:S(2)}) async-start(), calls=%async_computation.8 | async-start | bytes 3538944 | tf_op jit(solution)/shard_map/all_gather | solution.py:194
  10.3 387.4 %all-reduce.27.cloned.1.call-start = ((), (), s32[]{:S(2)}) async-start(), calls=%async_computation.23 | async-start | bytes 6291456 | tf_op jit(solution)/shard_map/psum | solution.py:273
  244.9 15.4 collective-permute-start.1
  246.2 14.1 collective-permute-start
  253.4 11.6 collective-permute-start.3
  254.7 10.3 collective-permute-start.2
  310.5 130.5 %all-gather.8.cloned.1.call-start = ((), (), s32[]{:S(2)}) async-start(), calls=%async_computation.9 | async-start | bytes 3538944 | tf_op jit(solution)/shard_map/all_gather | solution.py:198
  313.5 172.9 %all-gather.10.cloned.1.call-start = ((), (), s32[]{:S(2)}) async-start(), calls=%async_computation.10 | async-start | bytes 1769472 | tf_op jit(solution)/shard_map/all_gather | solution.py:199
  314.9 279.9 %all-reduce.25.cloned.1.call-start = ((), (), s32[]{:S(2)}) async-start(), calls=%async_computation.22 | async-start | bytes 6291456 | tf_op jit(solution)/shard_map/psum | solution.py:332
  527.2 232.8 %reduce-scatter.15.cloned.1.call-start = ((), (), s32[]{:S(2)}) async-start(), calls=%async_computation.11 | async-start | bytes 1769472 | tf_op jit(solution)/shard_map/reduce_scatter | solution.py:411
  662.1 136.8 %reduce-scatter.17.cloned.1.call-start = ((), (), s32[]{:S(2)}) async-start(), calls=%async_computation.12 | async-start | bytes 1769472 | tf_op jit(solution)/shard_map/reduce_scatter | solution.py:411
  676.8 40.5 %collective-permute-start.6 = (bf16[64,384]{0,1:T(8,128)(2,1)}, bf16[64,384]{0,1:T(8,128)(2,1)}, u32[]{:S(2)}, u32[]{:S(2)}) collective-permute-start(bf16[64,384]{0,1:T(8,128)(2,1)} %get-tuple-element.694), channel_id=1, source_target_pairs={{0,4},{4,8},{8,12},{12,16},{16,20},{20,24},{24,28},{1,5},{5,9},{9,... | collective-permute-start | bytes 147464 | tf_op jit(solution)/shard_map/ppermute | solution.py:33
  680.8 36.5 %collective-permute-start.7 = (bf16[64,384]{0,1:T(8,128)(2,1)}, bf16[64,384]{0,1:T(8,128)(2,1)}, u32[]{:S(2)}, u32[]{:S(2)}) collective-permute-start(bf16[64,384]{0,1:T(8,128)(2,1)} %get-tuple-element.695), channel_id=1, source_target_pairs={{4,0},{8,4},{12,8},{16,12},{20,16},{24,20},{28,24},{5,1},{9,5},{13... | collective-permute-start | bytes 147464 | tf_op jit(solution)/shard_map/ppermute | solution.py:35
  704.8 233.5 %all-reduce.23.cloned.1.call-start = ((), (), s32[]{:S(2)}) async-start(), calls=%async_computation.21 | async-start | bytes 12582912 | tf_op jit(solution)/shard_map/psum | solution.py:290
  710.8 16.7 collective-permute-start.4
  716.1 11.5 collective-permute-start.5
  818.9 186.5 %reduce-scatter.21.cloned.1.call-start = ((), (), s32[]{:S(2)}) async-start(), calls=%async_computation.14 | async-start | bytes 884736 | tf_op jit(solution)/shard_map/reduce_scatter | solution.py:459
  824.2 248.5 %reduce-scatter.19.cloned.1.call-start = ((), (), s32[]{:S(2)}) async-start(), calls=%async_computation.13 | async-start | bytes 1327104 | tf_op jit(solution)/shard_map/reduce_scatter | solution.py:457
  838.1 299.2 %reduce-scatter.29.cloned.1.call-start = ((), (), s32[]{:S(2)}) async-start(), calls=%async_computation.19 | async-start | bytes 442368
  860.7 354.6 %reduce-scatter.23.cloned.1.call-start = ((), (), s32[]{:S(2)}) async-start(), calls=%async_computation.15 | async-start | bytes 3538944 | tf_op jit(solution)/shard_map/reduce_scatter | solution.py:461
  865.0 610.1 %all-reduce.21.cloned.1.call-start = ((), (), s32[]{:S(2)}) async-start(), calls=%async_computation.20 | async-start | bytes 15728640
  890.7 648.8 %reduce-scatter.27.cloned.1.call-start = ((), (), s32[]{:S(2)}) async-start(), calls=%async_computation.18 | async-start | bytes 442368
  971.1 650.4 %reduce-scatter.25.cloned.1.call-start = ((), (), s32[]{:S(2)}) async-start(), calls=%async_computation.17 | async-start | bytes 3981312
  986.0 816.3 %all-reduce.19.cloned.1.call-start = ((), (), s32[]{:S(2)}) async-start(), calls=%async_computation.16 | async-start | bytes 147456 | tf_op jit(solution)/shard_map/psum | solution.py:521
  (294 other events, 5787.6 us)
Sparse Core Ops, SparseCore 0:
  10.8 63.0 all-gather.5
  310.6 66.9 all-reduce.26
  380.4 60.5 all-gather.7
  443.6 42.7 all-gather.9
  527.3 67.4 all-reduce.24
  662.2 68.0 reduce-scatter.14
  734.1 64.7 reduce-scatter.16
  819.0 119.1 all-reduce.22
  942.7 62.6 reduce-scatter.20
  1009.6 63.0 reduce-scatter.18
  1076.9 60.3 reduce-scatter.28
  1141.7 73.4 reduce-scatter.22
  1219.9 255.1 all-reduce.20
  1479.1 60.3 reduce-scatter.26
  1543.5 77.9 reduce-scatter.24
  1684.5 117.7 all-reduce.18
where the time goes:
time: 1910 us; the launch traced here: 1890 us
  waiting for transfers between devices  851 us (45%)
  other arithmetic  310 us (16%)
  blocking collectives  291 us (15%)
  local copies, waits for them, and re-layouts  220 us (12%)
  matrix products  172 us (9%)
  starting transfers between devices  25.9 us (1%)
  between operations  22.6 us (1%)
    unnamed x20, waiting for transfers between devices  444 us
    psum x1, waiting for transfers between devices, shards(): lax.psum((jnp.concatenate(row_parts), jnp.concatenate(col_parts), jnp.con...  102 us
    unnamed x619, local copies, waits for them, and re-layouts  78.5 us
    reduce_scatter x1, waiting for transfers between devices, shards(): lax.psum_scatter(totals[5], 'dp', scatter_dimension=0, tiled=True)  75.9 us
    reduce_scatter x1, waiting for transfers between devices, shards(): lax.psum_scatter(totals[1], 'dp', scatter_dimension=1, tiled=True)  65.6 us
    all_gather x2, blocking collectives, shards(): lax.all_gather(jnp.concatenate([heavy_key, scaled_value], axis=-1), 'dp',...  56.2 us
    psum x1, blocking collectives, shards(): update_sums = lax.psum(jnp.concatenate(update_parts), ('dp', 'mp'))  42 us
    psum x1, blocking collectives, shards(): lax.psum((jnp.concatenate(row_parts), jnp.concatenate(col_parts), jnp.con...  41.1 us
  transfers between devices with their start and end apart: 24, of which 13 were waited for; matrix products, arithmetic and copies ran while one was open for 22% of the time, Pallas kernels for 0%

commit v1 on v0

v1 whole, which is shorter than its diff:
```python
import functools
import math

import jax
import jax.numpy as jnp
from jax import lax
from jax.experimental import pallas as pl
from jax.experimental.pallas import tpu as pltpu
from jax.sharding import PartitionSpec as P

D = 768
LH = 8
LDH = 96
HH = 12
HDH = 64
WIN = 128
STEP = 10

norm_eps = 1e-06
tiny_square = 1e-30
scale_floor = 0.001
clip_level = 1.0
step_rate = 0.5
masked_score = -1e30
gelu_scale = math.sqrt(2.0 / math.pi)
gelu_cubic = 0.044715

low = jnp.bfloat16
wide = jnp.float32
CHUNK = 256
BLOCK = 128
RADIUS = WIN // 2
KEYS = 1024
VMEM_BYTES = 60 * 1024 * 1024


def nn(left, right):
    return lax.dot_general(left, right, (((1,), (0,)), ((), ())), preferred_element_type=wide)


def nt(left, right):
    return lax.dot_general(left, right, (((1,), (1,)), ((), ())), preferred_element_type=wide)


def tn(left, right):
    return lax.dot_general(left, right, (((0,), (0,)), ((), ())), preferred_element_type=wide)


def sigmoid(logit):
    return 1.0 / (1.0 + jnp.exp(-logit))


def gelu_pair(gate):
    squared = gate * gate
    bent = jnp.tanh(gelu_scale * gate * (1.0 + gelu_cubic * squared))
    half = 0.5 * (1.0 + bent)
    value = gate * half
    slope = half + 0.5 * gate * (1.0 - bent * bent) * gelu_scale * (1.0 + 3.0 * gelu_cubic * squared)
    return value, slope


def picks_rows(idx_col, count):
    spots = lax.broadcasted_iota(jnp.int32, (idx_col.shape[0], count), 1)
    return (spots == idx_col).astype(low)


def picks_cols(idx_row, start, count):
    spots = lax.broadcasted_iota(jnp.int32, (count, idx_row.shape[1]), 0) + start
    return (spots == idx_row).astype(low)


def head_mask(width, size, head):
    spot = lax.broadcasted_iota(jnp.int32, (1, width), 1)
    return ((spot >= head * size) & (spot < (head + 1) * size)).astype(low)


def softmax_parts(scores, allowed):
    masked = jnp.where(allowed, scores, masked_score)
    top = jnp.max(masked, axis=-1, keepdims=True)
    grown = jnp.exp(masked - top)
    return grown * (1.0 / jnp.sum(grown, axis=-1, keepdims=True))


def inverse_rms(values):
    return lax.rsqrt(jnp.mean(values * values, axis=-1, keepdims=True) + norm_eps)


def norm_back(values, gain_row, upstream):
    inverse = inverse_rms(values)
    unit = values * inverse
    scaled = upstream * gain_row
    pulled = inverse * (scaled - unit * jnp.mean(scaled * unit, axis=-1, keepdims=True))
    return pulled, jnp.sum(upstream * unit, axis=0, keepdims=True)


def in_vmem(shape, dtype):
    return jax.ShapeDtypeStruct(shape, dtype)


def kernel_call(body, outs, scratch, args, scalars=0, flops=0):
    vmem = pl.BlockSpec(memory_space=pltpu.VMEM)
    smem = pl.BlockSpec(memory_space=pltpu.SMEM)
    moved = sum(a.size * a.dtype.itemsize for a in args) + sum(
        math.prod(o.shape) * jnp.dtype(o.dtype).itemsize for o in outs
    )
    return pl.pallas_call(
        body,
        out_shape=outs,
        in_specs=[smem] * scalars + [vmem] * (len(args) - scalars),
        out_specs=[vmem] * len(outs),
        scratch_shapes=scratch,
        compiler_params=pltpu.CompilerParams(vmem_limit_bytes=VMEM_BYTES),
        cost_estimate=pl.CostEstimate(flops=flops, bytes_accessed=moved, transcendentals=0),
    )(*args)


def mp_total(core, first_ref, second_ref, near_ref, far_ref, chunk, per_half):
    rows = pl.ds(pl.multiple_of(chunk * CHUNK, CHUNK), CHUNK)
    mine = (first_ref[rows, :].astype(wide) + second_ref[rows, :].astype(wide)).astype(low)
    inner = pl.ds(pl.multiple_of((chunk % per_half) * CHUNK, CHUNK), CHUNK)
    flag = ((chunk // per_half) == core).astype(wide)
    other = near_ref[inner, :].astype(wide) * flag + far_ref[inner, :].astype(wide) * (1.0 - flag)
    return mine.astype(wide) + other


def unpack_body(got_ref, w_in_ref, w_out_ref, key_ref, vec_ref):
    count, _, lane = got_ref.shape
    in_rows = w_in_ref.shape[1] // count
    head_cols = w_in_ref.shape[2]
    for j in range(3):
        pair = got_ref[:, j * in_rows : (j + 1) * in_rows, :].reshape(count * in_rows, lane)
        w_in_ref[2 * j] = pair[:, :head_cols]
        w_in_ref[2 * j + 1] = pair[:, head_cols:]
    base = 3 * in_rows
    out_rows = w_out_ref.shape[1] // count
    sides = w_out_ref.shape[2] // lane
    for j in range(sides):
        cols = slice(j * lane, (j + 1) * lane)
        blocks = [
            got_ref[d, base + j * 2 * out_rows : base + (j + 1) * 2 * out_rows, :].astype(wide)
            for d in range(count)
        ]
        for s in range(2):
            w_out_ref[s, :, cols] = jnp.concatenate(
                [b[s * out_rows : (s + 1) * out_rows] for b in blocks], axis=0
            ).astype(low)
    base = base + 2 * out_rows * sides
    _, micros, quarter, _ = key_ref.shape
    for j in range(sides):
        cols = slice(j * lane, (j + 1) * lane)
        for m in range(micros):
            at = base + (j * micros + m) * quarter
            key_ref[:, m, :, cols] = got_ref[:, at : at + quarter, :]
    base = base + sides * micros * quarter
    vec_ref[...] = jnp.concatenate(
        [got_ref[d, base : base + 16, :].astype(wide)[:8, :in_rows] for d in range(count)], axis=1
    )


def block_of(ref, base, index, full):
    count = ref.shape[0]
    rows = full // count
    at = base // count + index * rows
    return ref[:, at : at + rows, :].reshape(full, CHUNK)


def part_of(ref, base, index, full, piece):
    count = ref.shape[0]
    rows = full // count
    at = base // count + index * rows
    if rows <= CHUNK:
        span = CHUNK // rows
        return ref[piece * span : (piece + 1) * span, at : at + rows, :].reshape(CHUNK, CHUNK)
    return ref[0, at + piece * CHUNK : at + (piece + 1) * CHUNK, :]


def ffn_bases(width, light, heavy):
    sides = width // CHUNK
    light_in = 2 * (light // CHUNK) * width
    light_out = sides * light
    heavy_in = 2 * (heavy // CHUNK) * width
    bases = [0, light_in, light_in + light_out, light_in + light_out + heavy_in]
    return bases, bases[3] + sides * heavy


def project_body(
    tok_ref, vec_ref, w_ref, qcol_ref, kcol_ref,
    n1b_ref, q_ref, k_ref, v_ref, hq_ref, sq_ref, nq_ref, nk_ref,
    qrows_ref, low_ref,
):
    count = tok_ref.shape[1]
    micros = tok_ref.shape[0]
    for m in range(micros):

        def step(c, carry):
            rows = pl.ds(pl.multiple_of(c * CHUNK, CHUNK), CHUNK)
            values = tok_ref[m, rows, :].astype(wide)
            normed = values * inverse_rms(values) * vec_ref[0:1, :]
            high = normed.astype(low)
            n1b_ref[m, rows, :] = high
            low_ref[rows, :] = (normed - high.astype(wide)).astype(low)
            q_ref[m, rows, :] = nn(high, w_ref[0]).astype(low)
            k_ref[m, rows, :] = nn(high, w_ref[1]).astype(low)
            v_ref[m, rows, :] = nn(high, w_ref[2]).astype(low)
            return carry

        lax.fori_loop(0, count // CHUNK, step, 0)
        picks = picks_rows(qcol_ref[m], count)
        query_rows = nn(picks, n1b_ref[m])
        query_wide = query_rows + nn(picks, low_ref[...])
        qrows_ref[m] = query_rows.astype(low)
        nq_ref[m] = query_wide
        hq_ref[m] = nn(query_rows.astype(low), w_ref[3]).astype(low)
        sq_ref[m] = sigmoid(jnp.sum(query_wide * vec_ref[2:3, :], axis=-1, keepdims=True))
        picks = picks_rows(kcol_ref[m], count)
        nk_ref[m] = nn(picks, n1b_ref[m]) + nn(picks, low_ref[...])


def keys_body(o_ref, a_ref, b_ref, c_ref, vec_ref, w_ref, n_ref, k_ref, v_ref, sk_ref):
    blocks, _, part, width = o_ref.shape
    for p, ref in enumerate((o_ref, a_ref, b_ref, c_ref)):
        values = ref[:, 0].reshape(blocks * part, width).astype(wide)
        normed = values * inverse_rms(values) * vec_ref[0:1, :]
        high = normed.astype(low)
        score = sigmoid(jnp.sum(normed * vec_ref[3:4, :], axis=-1, keepdims=True))
        n_ref[0, :, p] = high.reshape(blocks, part, width)
        sk_ref[0, :, p] = score.reshape(blocks, part, 1)
        k_ref[0, :, p] = nn(high, w_ref[4]).astype(low).reshape(blocks, part, -1)
        v_ref[0, :, p] = (nn(high, w_ref[5]) * score).astype(low).reshape(blocks, part, -1)


def fill_extended(ext_ref, prev, inner, after):
    count = inner.shape[0]
    ext_ref[0:RADIUS, :] = prev
    ext_ref[RADIUS : RADIUS + count, :] = inner
    ext_ref[RADIUS + count :, :] = after


def near_mask(seg_q, seg_k):
    shape = (BLOCK, 2 * BLOCK)
    gap = lax.broadcasted_iota(jnp.int32, shape, 1) - lax.broadcasted_iota(jnp.int32, shape, 0)
    return (gap >= 0) & (gap <= 2 * RADIUS) & (seg_q == seg_k)


def attend_body(
    q_ref, k_ref, v_ref, prev_ref, after_ref, hq_ref, hk_ref, hv_ref, sq_ref, wo_ref,
    qrow_ref, segq_ref, segk_ref, hsegq_ref, hsegk_ref,
    part_ref, lmix_ref, hmix_ref, hproj_ref,
    kx_ref, vx_ref, rows_ref,
):
    count, width = q_ref.shape
    light_heads = width // LDH
    heavy_heads = width // HDH
    fill_extended(kx_ref, prev_ref[0], k_ref[...], after_ref[0])
    fill_extended(vx_ref, prev_ref[1], v_ref[...], after_ref[1])
    allowed = hsegq_ref[...] == hsegk_ref[...]
    mix = jnp.zeros((hq_ref.shape[0], width), wide)
    for h in range(heavy_heads):
        mask = head_mask(width, HDH, h)
        probs = softmax_parts(nt(hq_ref[...], hk_ref[...] * mask) * (1.0 / math.sqrt(HDH)), allowed)
        mix = mix + nn(probs.astype(low), hv_ref[...] * mask)
    mix_low = mix.astype(low)
    hmix_ref[...] = mix_low
    proj = nn(mix_low, wo_ref[1])
    hproj_ref[...] = proj
    rows_ref[...] = (sq_ref[...] * proj).astype(low)

    def step(b, carry):
        rows = pl.ds(pl.multiple_of(b * BLOCK, BLOCK), BLOCK)
        keys = pl.ds(pl.multiple_of(b * BLOCK, BLOCK), 2 * BLOCK)
        seg_k = jnp.concatenate([segk_ref[b], segk_ref[b + 1]], axis=1)
        near = near_mask(segq_ref[rows, :], seg_k)
        queries = q_ref[rows, :]
        block_keys = kx_ref[keys, :]
        block_values = vx_ref[keys, :]
        total = jnp.zeros((BLOCK, width), wide)
        for h in range(light_heads):
            mask = head_mask(width, LDH, h)
            probs = softmax_parts(nt(queries, block_keys * mask) * (1.0 / math.sqrt(LDH)), near)
            total = total + nn(probs.astype(low), block_values * mask)
        total_low = total.astype(low)
        lmix_ref[rows, :] = total_low
        spread = picks_cols(qrow_ref[...], b * BLOCK, BLOCK)
        part_ref[rows, :] = (nn(total_low, wo_ref[0]) + nn(spread, rows_ref[...])).astype(low)
        return carry

    lax.fori_loop(0, count // BLOCK, step, 0)


def ffn_body(
    core_ref, first_ref, second_ref, near_ref, far_ref, tok_ref, cot_ref, vec_ref,
    fcol_ref, frow_ref, w_ref,
    middle_ref, y_ref, g_ref, n2b_ref, hidden_ref, dgu_ref, frows_ref, hhid_ref, dhgu_ref, dhout_ref,
    router_ref,
    low_ref, out_rows_ref, grad_rows_ref,
):
    count, width = tok_ref.shape
    chunks = count // CHUNK
    core = core_ref[0]
    light = hidden_ref.shape[1]
    heavy = hhid_ref.shape[1]
    sides = width // CHUNK
    bases, _ = ffn_bases(width, light, heavy)

    def heavy_in(s, j):
        return block_of(w_ref, bases[2], s * (heavy // CHUNK) + j, width)

    def heavy_out(t, j):
        return part_of(w_ref, bases[3], t, heavy, j)

    def light_in(s):
        return block_of(w_ref, bases[0], s, width)

    def light_out(t):
        return block_of(w_ref, bases[1], t, light)

    def enter(c, carry):
        rows = pl.ds(pl.multiple_of(c * CHUNK, CHUNK), CHUNK)
        middle = tok_ref[rows, :].astype(wide) + mp_total(
            core, first_ref, second_ref, near_ref, far_ref, c, chunks // 2
        )
        middle_ref[rows, :] = middle
        normed = middle * inverse_rms(middle) * vec_ref[1:2, :]
        high = normed.astype(low)
        n2b_ref[rows, :] = high
        low_ref[rows, :] = (normed - high.astype(wide)).astype(low)
        return carry

    lax.fori_loop(0, chunks, enter, 0)
    picks = picks_rows(fcol_ref[...], count)
    rows_high = nn(picks, n2b_ref[...])
    rows_wide = rows_high + nn(picks, low_ref[...])
    rows_low = rows_high.astype(low)
    frows_ref[...] = rows_low
    score = sigmoid(jnp.sum(rows_wide * vec_ref[4:5, :], axis=-1, keepdims=True))
    cot_rows = nn(picks, cot_ref[...])
    grad_out = (score * cot_rows).astype(low)
    dhout_ref[...] = grad_out
    out_rows = [jnp.zeros((rows_low.shape[0], CHUNK), wide) for _ in range(sides)]
    grad_rows = jnp.zeros(rows_low.shape, wide)
    for j in range(heavy // CHUNK):
        cols = slice(j * CHUNK, (j + 1) * CHUNK)
        gate = nn(rows_low, heavy_in(0, j))
        up = nn(rows_low, heavy_in(1, j))
        value, slope = gelu_pair(gate)
        hid = (value * up).astype(low)
        hhid_ref[:, cols] = hid
        grad_hid = jnp.zeros_like(gate)
        for t in range(sides):
            piece = heavy_out(t, j)
            out_rows[t] = out_rows[t] + nn(hid, piece)
            grad_hid = grad_hid + nt(grad_out[:, t * CHUNK : (t + 1) * CHUNK], piece)
        grad_gate = (grad_hid * up * slope).astype(low)
        grad_up = (grad_hid * value).astype(low)
        dhgu_ref[0, :, cols] = grad_gate
        dhgu_ref[1, :, cols] = grad_up
        grad_rows = grad_rows + nt(grad_gate, heavy_in(0, j)) + nt(grad_up, heavy_in(1, j))
    out_rows = jnp.concatenate(out_rows, axis=1)
    logit = jnp.sum(cot_rows * out_rows, axis=-1, keepdims=True) * score * (1.0 - score)
    router_ref[...] = jnp.sum(logit * rows_wide, axis=0, keepdims=True)
    out_rows_ref[...] = (score * out_rows).astype(low)
    grad_rows_ref[...] = (grad_rows + logit * vec_ref[4:5, :]).astype(low)

    def light_rows(c, carry):
        rows = pl.ds(pl.multiple_of(c * CHUNK, CHUNK), CHUNK)
        normed = n2b_ref[rows, :]
        gate = nn(normed, light_in(0))
        up = nn(normed, light_in(1))
        value, slope = gelu_pair(gate)
        hid = (value * up).astype(low)
        hidden_ref[rows, :] = hid
        spread = picks_cols(frow_ref[...], c * CHUNK, CHUNK)
        spread_out = nn(spread, out_rows_ref[...])
        grad_hid = jnp.zeros_like(gate)
        for t in range(sides):
            cols = slice(t * CHUNK, (t + 1) * CHUNK)
            y_ref[rows, cols] = (nn(hid, light_out(t)) + spread_out[:, cols]).astype(low)
            grad_hid = grad_hid + nt(cot_ref[rows, cols], light_out(t))
        grad_gate = (grad_hid * up * slope).astype(low)
        grad_up = (grad_hid * value).astype(low)
        dgu_ref[0, rows, :] = grad_gate
        dgu_ref[1, rows, :] = grad_up
        g_ref[rows, :] = (
            nt(grad_gate, light_in(0)) + nt(grad_up, light_in(1)) + nn(spread, grad_rows_ref[...])
        ).astype(low)
        return carry

    lax.fori_loop(0, chunks, light_rows, 0)


def ffn_grads_body(cot_ref, *refs):
    out_ref, turned_ref, rows_ref = refs[-3:]
    micros, tokens, width = cot_ref.shape
    groups = [refs[7 * m : 7 * m + 7] for m in range(micros)]
    count = out_ref.shape[0]
    light = groups[0][1].shape[1]
    heavy = groups[0][4].shape[1]
    routed = groups[0][3].shape[0]
    sides = width // CHUNK
    bases, _ = ffn_bases(width, light, heavy)

    def put(base, index, value):
        rows = value.shape[0] // count
        at = base // count + index * rows
        out_ref[:, at : at + rows, :] = value.astype(low).reshape(count, rows, CHUNK)

    light_out = jnp.zeros((light, width), wide)
    for m, group in enumerate(groups):
        turned_ref[:, m * tokens : (m + 1) * tokens] = group[0][...].T
        rows_ref[:, m * routed : (m + 1) * routed] = group[3][...].T
        light_out = light_out + tn(group[1][...], cot_ref[m])
    for t in range(sides):
        put(bases[1], t, light_out[:, t * CHUNK : (t + 1) * CHUNK])
    for s in range(2):
        total = jnp.zeros((width, CHUNK), wide)
        for m, group in enumerate(groups):
            total = total + nn(turned_ref[:, m * tokens : (m + 1) * tokens], group[2][s])
        put(bases[0], s, total)
    pieces = heavy // CHUNK
    for s in range(2):
        for j in range(pieces):
            total = jnp.zeros((width, CHUNK), wide)
            for m, group in enumerate(groups):
                total = total + nn(
                    rows_ref[:, m * routed : (m + 1) * routed],
                    group[5][s, :, j * CHUNK : (j + 1) * CHUNK],
                )
            put(bases[2], s * pieces + j, total)
    for t in range(sides):
        cols = slice(t * CHUNK, (t + 1) * CHUNK)
        total = jnp.zeros((heavy, CHUNK), wide)
        for m, group in enumerate(groups):
            total = total + tn(group[4][...], group[6][:, cols])
        put(bases[3], t, total)


def attend_back_body(
    core_ref, first_ref, second_ref, near_ref, far_ref, middle_ref, cot_ref, vec_ref,
    q_ref, k_ref, v_ref, prev_ref, after_ref, hq_ref, hk_ref, hv_ref, sk_ref, sq_ref, hproj_ref, wo_ref,
    qcol_ref, segq_ref, segk_ref, hsegq_ref, hsegk_ref,
    gmid_ref, agl_ref, gain_ref, dq_ref, inner_ref, edges_ref, dhq_ref, dhk_ref, dhv_ref, draw_ref,
    dproj_ref, logit_ref,
    kx_ref, vx_ref, dmix_ref, dkx_ref, dvx_ref,
):
    count, width = q_ref.shape
    chunks = count // CHUNK
    light_heads = width // LDH
    heavy_heads = width // HDH
    core = core_ref[0]
    fill_extended(kx_ref, prev_ref[0], k_ref[...], after_ref[0])
    fill_extended(vx_ref, prev_ref[1], v_ref[...], after_ref[1])
    gain_ref[...] = jnp.zeros_like(gain_ref)

    def enter(c, carry):
        rows = pl.ds(pl.multiple_of(c * CHUNK, CHUNK), CHUNK)
        upstream = mp_total(core, first_ref, second_ref, near_ref, far_ref, c, chunks // 2)
        pulled, gain = norm_back(middle_ref[rows, :], vec_ref[1:2, :], upstream)
        gain_ref[...] += gain
        grad_middle = cot_ref[rows, :].astype(wide) + pulled
        gmid_ref[rows, :] = grad_middle
        grad_low = grad_middle.astype(low)
        agl_ref[rows, :] = grad_low
        dmix_ref[rows, :] = nt(grad_low, wo_ref[0]).astype(low)
        return carry

    lax.fori_loop(0, chunks, enter, 0)

    picks = picks_rows(qcol_ref[...], count)
    grad_rows = nn(picks, agl_ref[...])
    score = sq_ref[...]
    dproj = (score * grad_rows).astype(low)
    dproj_ref[...] = dproj
    logit_ref[...] = (
        jnp.sum(grad_rows * hproj_ref[...], axis=-1, keepdims=True) * score * (1.0 - score)
    )
    dmix = nt(dproj, wo_ref[1]).astype(low)
    scale = 1.0 / math.sqrt(HDH)
    key_count = hk_ref.shape[0]
    if key_count <= KEYS:
        allowed = hsegq_ref[...] == hsegk_ref[...]
        dq = jnp.zeros((hq_ref.shape[0], width), wide)
        dk = jnp.zeros((key_count, width), wide)
        dv = jnp.zeros((key_count, width), wide)
        for h in range(heavy_heads):
            mask = head_mask(width, HDH, h)
            keys = hk_ref[...] * mask
            probs = softmax_parts(nt(hq_ref[...], keys) * scale, allowed)
            grad_soft = nt(dmix, hv_ref[...] * mask)
            centre = jnp.sum(probs * grad_soft, axis=-1, keepdims=True)
            grad_scores = (probs * (grad_soft - centre)).astype(low)
            dq = dq + nn(grad_scores, keys)
            dk = dk + tn(grad_scores, hq_ref[...] * mask)
            dv = dv + tn(probs.astype(low), dmix * mask)
        dhk_ref[...] = (dk * scale).astype(low)
        dhv_ref[...] = dv.astype(low)
        draw_ref[...] = (dv * sk_ref[...]).astype(low)
    else:
        pieces = key_count // KEYS

        def piece_of(c, mask):
            spots = pl.ds(pl.multiple_of(c * KEYS, KEYS), KEYS)
            allowed = hsegq_ref[...] == hsegk_ref[:, spots]
            keys = hk_ref[spots, :] * mask
            scores = jnp.where(allowed, nt(hq_ref[...], keys) * scale, masked_score)
            return spots, keys, scores, nt(dmix, hv_ref[spots, :] * mask)

        blank = jnp.zeros((hq_ref.shape[0], 1), wide)
        stats = []
        for h in range(heavy_heads):
            mask = head_mask(width, HDH, h)

            def find_top(c, top):
                return jnp.maximum(top, jnp.max(piece_of(c, mask)[2], axis=-1, keepdims=True))

            top = lax.fori_loop(0, pieces, find_top, blank + masked_score)

            def add_up(c, sums):
                _, _, scores, grad_soft = piece_of(c, mask)
                grown = jnp.exp(scores - top)
                return (
                    sums[0] + jnp.sum(grown, axis=-1, keepdims=True),
                    sums[1] + jnp.sum(grown * grad_soft, axis=-1, keepdims=True),
                )

            total, moment = lax.fori_loop(0, pieces, add_up, (blank, blank))
            stats.append((mask, top, 1.0 / total, moment / total))

        def pull(c, dq):
            dk = jnp.zeros((KEYS, width), wide)
            dv = jnp.zeros((KEYS, width), wide)
            for mask, top, inverse, centre in stats:
                spots, keys, scores, grad_soft = piece_of(c, mask)
                probs = jnp.exp(scores - top) * inverse
                grad_scores = (probs * (grad_soft - centre)).astype(low)
                dq = dq + nn(grad_scores, keys)
                dk = dk + tn(grad_scores, hq_ref[...] * mask)
                dv = dv + tn(probs.astype(low), dmix * mask)
            dhk_ref[spots, :] = (dk * scale).astype(low)
            dhv_ref[spots, :] = dv.astype(low)
            draw_ref[spots, :] = (dv * sk_ref[spots, :]).astype(low)
            return dq

        dq = lax.fori_loop(0, pieces, pull, jnp.zeros((hq_ref.shape[0], width), wide))
    dhq_ref[...] = (dq * scale).astype(low)

    dkx_ref[...] = jnp.zeros_like(dkx_ref)
    dvx_ref[...] = jnp.zeros_like(dvx_ref)
    light_scale = 1.0 / math.sqrt(LDH)

    def step(b, carry):
        rows = pl.ds(pl.multiple_of(b * BLOCK, BLOCK), BLOCK)
        spans = pl.ds(pl.multiple_of(b * BLOCK, BLOCK), 2 * BLOCK)
        seg_k = jnp.concatenate([segk_ref[b], segk_ref[b + 1]], axis=1)
        near = near_mask(segq_ref[rows, :], seg_k)
        queries = q_ref[rows, :]
        block_keys = kx_ref[spans, :]
        block_values = vx_ref[spans, :]
        mix = dmix_ref[rows, :]
        grad_q = jnp.zeros((BLOCK, width), wide)
        grad_k = jnp.zeros((2 * BLOCK, width), wide)
        grad_v = jnp.zeros((2 * BLOCK, width), wide)
        for h in range(light_heads):
            mask = head_mask(width, LDH, h)
            keys = block_keys * mask
            probs = softmax_parts(nt(queries, keys) * light_scale, near)
            grad_soft = nt(mix, block_values * mask)
            centre = jnp.sum(probs * grad_soft, axis=-1, keepdims=True)
            grad_scores = (probs * (grad_soft - centre)).astype(low)
            grad_q = grad_q + nn(grad_scores, keys)
            grad_k = grad_k + tn(grad_scores, queries * mask)
            grad_v = grad_v + tn(probs.astype(low), mix * mask)
        dq_ref[rows, :] = (grad_q * light_scale).astype(low)
        dkx_ref[spans, :] += grad_k * light_scale
        dvx_ref[spans, :] += grad_v
        return carry

    lax.fori_loop(0, count // BLOCK, step, 0)
    for s, ref in enumerate((dkx_ref, dvx_ref)):
        inner_ref[s] = ref[RADIUS : RADIUS + count, :]
        edges_ref[0, s] = ref[RADIUS + count :, :].astype(low)
        edges_ref[1, s] = ref[:RADIUS, :].astype(low)


def project_back_body(
    dq_ref, inner_ref, prev_ref, after_ref, dhq_ref, logit_ref, owned_ref, nq_ref, nk_ref, vec_ref, w_ref,
    qrow_ref, krow_ref,
    part_ref, dkv_ref, router_ref,
    rows_ref,
):
    count, width = dq_ref.shape
    routed = dhq_ref.shape[0]
    sources = owned_ref.shape[0]
    for s in range(2):
        dkv_ref[s, RADIUS : count - RADIUS, :] = inner_ref[s, RADIUS : count - RADIUS, :].astype(low)
        dkv_ref[s, :RADIUS, :] = (inner_ref[s, :RADIUS, :] + prev_ref[s].astype(wide)).astype(low)
        dkv_ref[s, count - RADIUS :, :] = (
            inner_ref[s, count - RADIUS :, :] + after_ref[s].astype(wide)
        ).astype(low)
    owned = owned_ref[0].astype(wide)
    for s in range(1, sources):
        owned = owned + owned_ref[s].astype(wide)
    grad_k = owned[:, :width]
    grad_v = owned[:, width:]
    grad_v = grad_v.astype(low).astype(wide)
    key_wide = nk_ref[...]
    raw = nn(key_wide.astype(low), w_ref[5])
    score = sigmoid(jnp.sum(key_wide * vec_ref[3:4, :], axis=-1, keepdims=True))
    key_logit = jnp.sum(grad_v * raw, axis=-1, keepdims=True) * score * (1.0 - score)
    grad_raw = (grad_v * score).astype(low)
    query_logit = logit_ref[...]
    router_ref[0:1, :] = jnp.sum(query_logit * nq_ref[...], axis=0, keepdims=True)
    router_ref[1:2, :] = jnp.sum(key_logit * key_wide, axis=0, keepdims=True)
    rows_ref[0:routed, :] = (nt(dhq_ref[...], w_ref[3]) + query_logit * vec_ref[2:3, :]).astype(low)
    rows_ref[routed:, :] = (
        nt(grad_k.astype(low), w_ref[4]) + nt(grad_raw, w_ref[5]) + key_logit * vec_ref[3:4, :]
    ).astype(low)

    def step(c, carry):
        rows = pl.ds(pl.multiple_of(c * CHUNK, CHUNK), CHUNK)
        spread = jnp.concatenate(
            [picks_cols(qrow_ref[...], c * CHUNK, CHUNK), picks_cols(krow_ref[...], c * CHUNK, CHUNK)],
            axis=1,
        )
        part_ref[rows, :] = (
            nt(dq_ref[rows, :], w_ref[0])
            + nt(dkv_ref[0, rows, :], w_ref[1])
            + nt(dkv_ref[1, rows, :], w_ref[2])
            + nn(spread, rows_ref[...])
        ).astype(low)
        return carry

    lax.fori_loop(0, count // CHUNK, step, 0)


def finish_body(core_ref, *refs):
    micros = (len(refs) - 4) // 5
    pieces = refs[: 4 * micros]
    grads = refs[4 * micros : 5 * micros]
    tok_ref, vec_ref, out_ref, gain_ref = refs[5 * micros :]
    chunks = tok_ref.shape[1] // CHUNK
    core = core_ref[0]
    gain_ref[...] = jnp.zeros_like(gain_ref)
    for m in range(micros):
        first_ref, second_ref, near_ref, far_ref = pieces[4 * m : 4 * m + 4]

        def step(c, carry):
            rows = pl.ds(pl.multiple_of(c * CHUNK, CHUNK), CHUNK)
            upstream = mp_total(core, first_ref, second_ref, near_ref, far_ref, c, chunks // 2)
            pulled, gain = norm_back(tok_ref[m, rows, :].astype(wide), vec_ref[0:1, :], upstream)
            gain_ref[...] += gain
            out_ref[m, rows, :] = grads[m][rows, :] + pulled
            return carry

        lax.fori_loop(0, chunks, step, 0)


def join_body(core_ref, *refs):
    out_ref = refs[-1]
    micros = out_ref.shape[0]
    chunks = out_ref.shape[1] // CHUNK
    core = core_ref[0]
    for m in range(micros):
        middle_ref, first_ref, second_ref, near_ref, far_ref = refs[5 * m : 5 * m + 5]

        def step(c, carry):
            rows = pl.ds(pl.multiple_of(c * CHUNK, CHUNK), CHUNK)
            total = mp_total(core, first_ref, second_ref, near_ref, far_ref, c, chunks // 2)
            out_ref[m, rows, :] = (middle_ref[rows, :] + total).astype(low)
            return carry

        lax.fori_loop(0, chunks, step, 0)


def attn_grads_body(normed_ref, query_ref, key_ref, *refs):
    micros, tokens, width = normed_ref.shape
    outs = refs[9 * micros : -2]
    turned_ref, other_ref = refs[-2:]
    groups = [refs[9 * m : 9 * m + 9] for m in range(micros)]
    keys = key_ref.shape[1]
    grads = []
    for m in range(micros):
        turned_ref[:, m * tokens : (m + 1) * tokens] = normed_ref[m].T
    for s in range(3):
        total = 0.0
        for m, group in enumerate(groups):
            grad = group[0][...] if s == 0 else group[1][s - 1]
            total = total + nn(turned_ref[:, m * tokens : (m + 1) * tokens], grad)
        grads.append(total)
    total = 0.0
    for m, group in enumerate(groups):
        total = total + tn(query_ref[m], group[2][...])
    grads.append(total)
    for m in range(micros):
        other_ref[:, m * keys : (m + 1) * keys] = key_ref[m].T
    for s in (3, 4):
        total = 0.0
        for m, group in enumerate(groups):
            total = total + nn(other_ref[:, m * keys : (m + 1) * keys], group[s][...])
        grads.append(total)
    out_grads = []
    for mix, grad in ((5, 6), (7, 8)):
        total = 0.0
        for group in groups:
            total = total + tn(group[mix][...], group[grad][...])
        out_grads.append(total)
    (out_ref,) = outs
    count, _, lane = out_ref.shape
    in_rows = width // count
    for j in range(3):
        pair = jnp.concatenate([grads[2 * j], grads[2 * j + 1]], axis=1).astype(low)
        out_ref[:, j * in_rows : (j + 1) * in_rows, :] = pair.reshape(count, in_rows, lane)
    out_rows = out_grads[0].shape[0] // count
    for d in range(count):
        rows = slice(d * out_rows, (d + 1) * out_rows)
        both = jnp.concatenate([g[rows] for g in out_grads], axis=0).astype(low)
        for j in range(width // lane):
            at = 3 * in_rows + j * 2 * out_rows
            out_ref[d, at : at + 2 * out_rows, :] = both[:, j * lane : (j + 1) * lane]


def scaled_step(weight, update, weight_sum, update_sum, count_all, lead_shape):
    rms_weight = jnp.sqrt(weight_sum / count_all).reshape(lead_shape)
    rms_update = jnp.sqrt(update_sum / count_all).reshape(lead_shape)
    step_size = (
        step_rate * jnp.maximum(scale_floor, rms_weight) / jnp.maximum(1.0, rms_update / clip_level)
    )
    return weight - step_size * update


def after(value, *others):
    return lax.optimization_barrier((value,) + others)[0]


def shards(
    tokens,
    cotangent,
    segments,
    route_query,
    route_key,
    route_ffn,
    attn_in,
    attn_out,
    light_in,
    light_out,
    heavy_in,
    heavy_out,
    gains,
    router,
    row_attn_in,
    col_attn_in,
    row_attn_out,
    col_attn_out,
    row_light_in,
    col_light_in,
    row_light_out,
    col_light_out,
    row_heavy_in,
    col_heavy_in,
    row_heavy_out,
    col_heavy_out,
    second_gains,
    second_router,
):
    data_size = lax.axis_size("dp")
    model_size = lax.axis_size("mp")
    data_index = lax.axis_index("dp")
    model_index = lax.axis_index("mp")
    core = model_index % 2
    core_flag = core.astype(jnp.int32).reshape(1)
    core_pairs = [(i, i ^ 1) for i in range(model_size)]
    far_pairs = [(i, i ^ 2) for i in range(model_size)]
    micro_count, tok_local, width = tokens.shape
    routed_local = route_query.shape[1]
    routed_all = route_key.shape[1]
    quarter = routed_local // model_size
    head_cols = attn_in.shape[2]
    in_rows = attn_in.shape[1]

    order = jnp.arange(model_size) ^ model_index
    key_blocks = route_key.reshape(micro_count, data_size, model_size, quarter)
    key_blocks = jnp.take(key_blocks, order, axis=2)
    key_local = lax.dynamic_slice_in_dim(key_blocks, data_index, 1, axis=1)[:, 0]
    my_quarter = key_local[:, 0]
    picks = (my_quarter[:, :, None] == jnp.arange(tok_local)[None, None, :]).astype(low)
    my_rows = jnp.einsum("mrt,mtd->mrd", picks, tokens, preferred_element_type=wide).astype(low)

    lane = 2 * head_cols
    sides = width // lane
    out_rows = attn_out.shape[1]
    small = jnp.concatenate([gains, router], axis=0).astype(low)
    small_block = jnp.pad(small, ((0, 16 - small.shape[0]), (0, lane - in_rows)))
    in_block = (
        attn_in.astype(low).reshape(3, 2, in_rows, head_cols).transpose(0, 2, 1, 3).reshape(3 * in_rows, lane)
    )

    def sideways(rows):
        return rows.reshape(-1, sides, lane).transpose(1, 0, 2).reshape(-1, lane)

    out_block = sideways(attn_out.astype(low).reshape(2 * out_rows, width))
    key_block = sideways(my_rows.reshape(-1, width))
    pack_one = jnp.concatenate([in_block, out_block, key_block, small_block], axis=0)
    got_one = lax.all_gather(pack_one, "dp", axis=0, tiled=False)
    aligned = in_rows % 16 == 0 and out_rows % 8 == 0 and light_out.shape[0] % 16 == 0
    if aligned:
        w_in, w_out, key_rows, vectors = kernel_call(
            unpack_body,
            [
                in_vmem((6, width, head_cols), low),
                in_vmem((2, data_size * out_rows, width), low),
                in_vmem((data_size, micro_count, quarter, width), low),
                in_vmem((8, width), wide),
            ],
            [],
            (got_one,),
        )
    else:
        w_in = (
            got_one[:, : 3 * in_rows]
            .reshape(data_size, 3, in_rows, 2, head_cols)
            .transpose(1, 3, 0, 2, 4)
            .reshape(6, width, head_cols)
        )
        at = 3 * in_rows
        w_out = (
            got_one[:, at : at + out_block.shape[0]]
            .reshape(data_size, sides, 2, out_rows, lane)
            .transpose(2, 0, 3, 1, 4)
            .reshape(2, data_size * out_rows, width)
        )
        at = at + out_block.shape[0]
        key_rows = (
            got_one[:, at : at + key_block.shape[0]]
            .reshape(data_size, sides, micro_count, quarter, lane)
            .transpose(0, 2, 3, 1, 4)
            .reshape(data_size, micro_count, quarter, width)
        )
        at = at + key_block.shape[0]
        vectors = got_one[:, at : at + 8, :in_rows].transpose(1, 0, 2).reshape(8, width).astype(wide)

    def blocked(weight):
        lead, rows, cols = weight.shape
        return weight.reshape(lead, rows, cols // CHUNK, CHUNK).transpose(0, 2, 1, 3).reshape(-1, rows, CHUNK)

    def unblocked(blocks, lead):
        count, rows, _ = blocks.shape
        return blocks.reshape(lead, count // lead, rows, CHUNK).transpose(0, 2, 1, 3).reshape(lead, rows, -1)

    light_hidden = light_in.shape[2]
    heavy_hidden = heavy_in.shape[2]
    blocks = [blocked(w.astype(low)) for w in (light_in, light_out[None], heavy_in, heavy_out[None])]
    block_rows = [b.shape[0] * b.shape[1] for b in blocks]
    pack_two = jnp.concatenate([b.reshape(-1, CHUNK) for b in blocks], axis=0)
    pack_two = after(pack_two, got_one)
    w_ffn = lax.all_gather(pack_two, "dp", axis=0, tiled=False)
    if not aligned:
        pieces = []
        at = 0
        for block in blocks:
            size = block.shape[0] * block.shape[1]
            pieces.append(
                w_ffn[:, at : at + size]
                .reshape((data_size,) + block.shape)
                .transpose(1, 0, 2, 3)
                .reshape(-1, CHUNK)
            )
            at = at + size
        w_ffn = jnp.concatenate(pieces, axis=0)[None]

    turns = (jnp.arange(micro_count) % 2)[:, None]
    segment_ids = segments[None, :] * turns
    seg_padded = jnp.pad(segment_ids, ((0, 0), (RADIUS, RADIUS)), constant_values=-1)
    seg_local = lax.dynamic_slice_in_dim(segment_ids, data_index * tok_local, tok_local, axis=1)
    seg_extended = lax.dynamic_slice_in_dim(
        seg_padded, data_index * tok_local, tok_local + 2 * RADIUS, axis=1
    ).reshape(micro_count, -1, 1, BLOCK)

    def picked(ids, spots):
        hit = spots[..., :, None] == jnp.arange(tok_local)
        return jnp.sum(jnp.where(hit, ids[..., None, :], 0), axis=-1)

    key_seg = picked(
        segment_ids.reshape(micro_count, data_size, tok_local),
        key_blocks.reshape(micro_count, data_size, routed_local),
    ).reshape(micro_count, -1)
    query_seg = picked(seg_local, route_query)
    key_list = key_local.reshape(micro_count, -1)

    project_outs = [
        in_vmem((micro_count, tok_local, width), low),
        in_vmem((micro_count, tok_local, head_cols), low),
        in_vmem((micro_count, tok_local, head_cols), low),
        in_vmem((micro_count, tok_local, head_cols), low),
        in_vmem((micro_count, routed_local, head_cols), low),
        in_vmem((micro_count, routed_local, 1), wide),
        in_vmem((micro_count, routed_local, width), wide),
        in_vmem((micro_count, routed_local, width), wide),
        in_vmem((micro_count, routed_local, width), low),
    ]
    normed_low, light_q, light_k, light_v, heavy_q, score_q, rows_q, rows_k, rows_q_low = kernel_call(
        project_body,
        project_outs,
        [pltpu.VMEM((tok_local, width), low)],
        (tokens, vectors, w_in, route_query[:, :, None], key_list[:, :, None]),
        flops=5_000_000_000,
    )

    up = [(i, i + 1) for i in range(data_size - 1)]
    down = [(i + 1, i) for i in range(data_size - 1)]
    light_kv = (light_k, light_v)
    tails = jnp.stack([a[:, tok_local - RADIUS :] for a in light_kv], axis=1)
    heads = jnp.stack([a[:, :RADIUS] for a in light_kv], axis=1)
    halo_prev = lax.ppermute(tails, "dp", up)
    halo_next = lax.ppermute(heads, "dp", down)

    rows_core = lax.ppermute(key_rows, "mp", core_pairs)
    rows_far = lax.ppermute(key_rows, "mp", far_pairs)
    rows_both = lax.ppermute(rows_far, "mp", core_pairs)
    split = (micro_count, data_size, model_size, quarter)
    span = min(data_size, 8)
    row_spec = pl.BlockSpec((span, 1, quarter, width), lambda m, i: (i, m, 0, 0))

    def split_spec(cols):
        return pl.BlockSpec((1, span, model_size, quarter, cols), lambda m, i: (m, i, 0, 0, 0))

    key_normed, heavy_k, heavy_v, score_k = pl.pallas_call(
        keys_body,
        grid=(micro_count, data_size // span),
        out_shape=[
            in_vmem(split + (width,), low),
            in_vmem(split + (head_cols,), low),
            in_vmem(split + (head_cols,), low),
            in_vmem(split + (1,), wide),
        ],
        in_specs=[row_spec] * 4
        + [
            pl.BlockSpec((8, width), lambda m, i: (0, 0)),
            pl.BlockSpec((6, width, head_cols), lambda m, i: (0, 0, 0)),
        ],
        out_specs=[split_spec(width), split_spec(head_cols), split_spec(head_cols), split_spec(1)],
        compiler_params=pltpu.CompilerParams(vmem_limit_bytes=VMEM_BYTES),
        cost_estimate=pl.CostEstimate(flops=10_000_000_000, bytes_accessed=10_000_000, transcendentals=0),
    )(key_rows, rows_core, rows_far, rows_both, vectors, w_in)
    key_normed = key_normed.reshape(micro_count, routed_all, width)
    heavy_k = heavy_k.reshape(micro_count, routed_all, head_cols)
    heavy_v = heavy_v.reshape(micro_count, routed_all, head_cols)
    score_k = score_k.reshape(micro_count, routed_all, 1)

    half_rows = tok_local // 2

    def mp_sum(part):
        second = lax.ppermute(part, "mp", core_pairs)
        mine = lax.dynamic_slice_in_dim(part, core * half_rows, half_rows, 0).astype(wide)
        theirs = lax.dynamic_slice_in_dim(second, core * half_rows, half_rows, 0).astype(wide)
        near = lax.ppermute((mine + theirs).astype(low), "mp", far_pairs)
        far = lax.ppermute(near, "mp", core_pairs)
        return part, second, near, far

    extended = pltpu.VMEM((tok_local + 2 * RADIUS, head_cols), low)
    row_shape = (tok_local, width)
    attended = []
    for m in range(micro_count):
        segs = (
            seg_local[m][:, None],
            seg_extended[m],
            query_seg[m][:, None],
            key_seg[m][None, :],
        )
        part, light_mix, heavy_mix, heavy_proj = kernel_call(
            attend_body,
            [
                in_vmem(row_shape, low),
                in_vmem((tok_local, head_cols), low),
                in_vmem((routed_local, head_cols), low),
                in_vmem((routed_local, width), wide),
            ],
            [extended, extended, pltpu.VMEM((routed_local, width), low)],
            (
                light_q[m], light_k[m], light_v[m], halo_prev[m], halo_next[m], heavy_q[m], heavy_k[m],
                heavy_v[m], score_q[m], w_out, route_query[m][None, :],
            )
            + segs,
            flops=4_000_000_000,
        )
        attended.append((segs, light_mix, heavy_mix, heavy_proj, mp_sum(part)))

    fed = []
    for m in range(micro_count):
        outs = kernel_call(
            ffn_body,
            [
                in_vmem(row_shape, wide),
                in_vmem(row_shape, low),
                in_vmem(row_shape, low),
                in_vmem(row_shape, low),
                in_vmem((tok_local, light_hidden), low),
                in_vmem((2, tok_local, light_hidden), low),
                in_vmem((routed_local, width), low),
                in_vmem((routed_local, heavy_hidden), low),
                in_vmem((2, routed_local, heavy_hidden), low),
                in_vmem((routed_local, width), low),
                in_vmem((1, width), wide),
            ],
            [
                pltpu.VMEM(row_shape, low),
                pltpu.VMEM((routed_local, width), low),
                pltpu.VMEM((routed_local, width), low),
            ],
            (core_flag,)
            + attended[m][4]
            + (
                tokens[m], cotangent[m], vectors, route_ffn[m][:, None], route_ffn[m][None, :], w_ffn,
            ),
            scalars=1,
            flops=6_000_000_000,
        )
        fed.append(tuple(outs) + (mp_sum(outs[2]),))

    grad_args = (cotangent,)
    for m in range(micro_count):
        grad_args = grad_args + tuple(fed[m][3:10])
    total_rows = ffn_bases(width, light_hidden, heavy_hidden)[1]
    split = data_size if aligned else 1
    (pack_ffn,) = kernel_call(
        ffn_grads_body,
        [in_vmem((split, total_rows // split, CHUNK), low)],
        [
            pltpu.VMEM((width, micro_count * tok_local), low),
            pltpu.VMEM((width, micro_count * routed_local), low),
        ],
        grad_args,
        flops=4_000_000_000,
    )
    if not aligned:
        pieces = []
        at = 0
        for block in blocks:
            size = block.shape[0] * block.shape[1] * data_size
            pieces.append(
                pack_ffn[0, at : at + size]
                .reshape(block.shape[0], data_size, block.shape[1], CHUNK)
                .transpose(1, 0, 2, 3)
                .reshape(data_size, -1, CHUNK)
            )
            at = at + size
        pack_ffn = jnp.concatenate(pieces, axis=1)
    sum_ffn = lax.psum_scatter(pack_ffn.reshape(-1, CHUNK), "dp", scatter_dimension=0, tiled=True)
    y_moved = []
    held = fed[-1][11][2]
    for m in range(micro_count):
        moved = mp_sum(after(fed[m][1], held))
        held = moved[2]
        y_moved.append(moved)

    backs = []
    for m in range(micro_count):
        segs, light_mix, heavy_mix, heavy_proj, _ = attended[m]
        outs = kernel_call(
            attend_back_body,
            [
                in_vmem(row_shape, wide),
                in_vmem(row_shape, low),
                in_vmem((1, width), wide),
                in_vmem((tok_local, head_cols), low),
                in_vmem((2, tok_local, head_cols), wide),
                in_vmem((2, 2, RADIUS, head_cols), low),
                in_vmem((routed_local, head_cols), low),
                in_vmem((routed_all, head_cols), low),
                in_vmem((routed_all, head_cols), low),
                in_vmem((routed_all, head_cols), low),
                in_vmem((routed_local, width), low),
                in_vmem((routed_local, 1), wide),
            ],
            [
                extended,
                extended,
                pltpu.VMEM((tok_local, head_cols), low),
                pltpu.VMEM((tok_local + 2 * RADIUS, head_cols), wide),
                pltpu.VMEM((tok_local + 2 * RADIUS, head_cols), wide),
            ],
            (core_flag,)
            + fed[m][11]
            + (
                fed[m][0], cotangent[m], vectors, light_q[m], light_k[m], light_v[m], halo_prev[m],
                halo_next[m], heavy_q[m], heavy_k[m], heavy_v[m], score_k[m], score_q[m], heavy_proj,
                w_out, route_query[m][:, None],
            )
            + segs,
            scalars=1,
            flops=8_000_000_000,
        )
        spread = jnp.concatenate([outs[7], outs[8]], axis=1).reshape(data_size, routed_local, 2 * head_cols)
        owned = lax.all_to_all(spread, "dp", 0, 0, tiled=True)
        backs.append((outs, owned))
    edges = jnp.stack([backs[m][0][5] for m in range(micro_count)], axis=1)
    from_prev = lax.ppermute(edges[0], "dp", up)
    from_next = lax.ppermute(edges[1], "dp", down)

    last = []
    for m in range(micro_count):
        outs, owned = backs[m]
        part, grads_kv, router_part = kernel_call(
            project_back_body,
            [
                in_vmem(row_shape, low),
                in_vmem((2, tok_local, head_cols), low),
                in_vmem((2, width), wide),
            ],
            [pltpu.VMEM((2 * routed_local, width), low)],
            (
                outs[3], outs[4], from_prev[m], from_next[m], outs[6], outs[11], owned, rows_q[m], rows_k[m],
                vectors, w_in, route_query[m][None, :], key_list[m][None, :],
            ),
            flops=3_000_000_000,
        )
        last.append((mp_sum(part), grads_kv, router_part))

    attn_rows = 3 * in_rows + 2 * out_rows * sides
    groups = []
    for m in range(micro_count):
        outs = backs[m][0]
        groups.append(
            (outs[3], last[m][1], outs[6], outs[7], outs[9], attended[m][1], outs[1], attended[m][2], outs[10])
        )
    if aligned:
        (pack_attn,) = kernel_call(
            attn_grads_body,
            [in_vmem((data_size, attn_rows, lane), low)],
            [
                pltpu.VMEM((width, micro_count * tok_local), low),
                pltpu.VMEM((width, micro_count * routed_all), low),
            ],
            (normed_low, rows_q_low, key_normed) + sum(groups, ()),
            flops=4_000_000_000,
        )
    else:
        totals = [0.0] * 8
        for m, group in enumerate(groups):
            pairs = (
                (normed_low[m], group[0]), (normed_low[m], group[1][0]), (normed_low[m], group[1][1]),
                (rows_q_low[m], group[2]), (key_normed[m], group[3]), (key_normed[m], group[4]),
                (group[5], group[6]), (group[7], group[8]),
            )
            totals = [total + tn(left, right) for total, (left, right) in zip(totals, pairs)]
        grad_in = jnp.stack(totals[:6]).astype(low)
        grad_out = jnp.stack(totals[6:]).astype(low)
        pack_attn = jnp.concatenate(
            [
                grad_in.reshape(3, 2, data_size, in_rows, head_cols)
                .transpose(2, 0, 3, 1, 4)
                .reshape(data_size, 3 * in_rows, lane),
                grad_out.reshape(2, data_size, out_rows, sides, lane)
                .transpose(1, 3, 0, 2, 4)
                .reshape(data_size, -1, lane),
            ],
            axis=1,
        )
    pack_attn = after(pack_attn.reshape(-1, lane), sum_ffn)
    sum_attn = lax.psum_scatter(pack_attn, "dp", scatter_dimension=0, tiled=True)

    join_args = ()
    for m in range(micro_count):
        join_args = join_args + (fed[m][0],) + y_moved[m]
    (mixed,) = kernel_call(
        join_body, [in_vmem(tokens.shape, low)], [], (core_flag,) + join_args, scalars=1
    )
    pieces = ()
    for m in range(micro_count):
        pieces = pieces + last[m][0]
    grad_tokens, gain_one = kernel_call(
        finish_body,
        [in_vmem(tokens.shape, wide), in_vmem((1, width), wide)],
        [],
        (core_flag,) + pieces + tuple(backs[m][0][0] for m in range(micro_count)) + (tokens, vectors),
        scalars=1,
    )
    gain_two = sum(backs[m][0][2] for m in range(micro_count))
    router_low = sum(last[m][2] for m in range(micro_count))
    router_ffn = sum(fed[m][10] for m in range(micro_count))
    vector_grads = jnp.concatenate(
        [gain_one / model_size, gain_two / model_size, router_low, router_ffn], axis=0
    )

    grad_attn_in = (
        sum_attn[: 3 * in_rows]
        .reshape(3, in_rows, 2, head_cols)
        .transpose(0, 2, 1, 3)
        .reshape(6, in_rows, head_cols)
        .astype(wide)
    )
    grad_attn_out = (
        sum_attn[3 * in_rows :]
        .reshape(sides, 2, out_rows, lane)
        .transpose(1, 2, 0, 3)
        .reshape(2, out_rows, width)
        .astype(wide)
    )
    ffn_grads = []
    at = 0
    for weight, block, size in zip((light_in, light_out, heavy_in, heavy_out), blocks, block_rows):
        lead = weight.size // (weight.shape[-1] * weight.shape[-2])
        ffn_grads.append(
            unblocked(sum_ffn[at : at + size].reshape(block.shape), lead).reshape(weight.shape).astype(wide)
        )
        at = at + size
    reduced = [grad_attn_in, grad_attn_out] + ffn_grads

    device_count = data_size * model_size

    def all_parts(values):
        sent = jnp.broadcast_to(values[None, :], (device_count, values.shape[0]))
        return lax.all_to_all(sent, ("dp", "mp"), 0, 0, tiled=True)

    local_spot = model_index * data_size + data_index
    specs = (
        (attn_in, reduced[0], row_attn_in, col_attn_in, data_index * attn_in.shape[-2], model_index * attn_in.shape[-1]),
        (attn_out, reduced[1], row_attn_out, col_attn_out, local_spot * attn_out.shape[-2], 0),
        (light_in, reduced[2], row_light_in, col_light_in, data_index * light_in.shape[-2], model_index * light_in.shape[-1]),
        (light_out, reduced[3], row_light_out, col_light_out, local_spot * light_out.shape[-2], 0),
        (heavy_in, reduced[4], row_heavy_in, col_heavy_in, data_index * heavy_in.shape[-2], model_index * heavy_in.shape[-1]),
        (heavy_out, reduced[5], row_heavy_out, col_heavy_out, local_spot * heavy_out.shape[-2], 0),
    )
    tall = (True, False, True, False, True, False)
    decay_rate = 1.0 - STEP ** (-0.8)

    def updated(chosen, vectors_too):
        parts = []
        for index in chosen:
            weight, gradient = specs[index][:2]
            square = gradient * gradient + tiny_square
            parts.append(jnp.sum(square, axis=-1).reshape(-1))
            parts.append(jnp.sum(square, axis=-2).reshape(-1))
            parts.append(jnp.sum(weight * weight, axis=(-2, -1)).reshape(-1))
        if vectors_too:
            parts.append(jnp.sum(gains * gains, axis=-1) / model_size)
            parts.append(jnp.sum(router * router, axis=-1) / model_size)
            parts.append(vector_grads.reshape(-1))
        starts = [0]
        for part in parts:
            starts.append(starts[-1] + part.shape[0])
        packed = jnp.pad(jnp.concatenate(parts), (0, -starts[-1] % 1024))
        gathered = all_parts(packed).reshape(data_size, model_size, -1)

        def section(place):
            return gathered[:, :, starts[place] : starts[place + 1]]

        pending = []
        update_parts = []
        for place, index in enumerate(chosen):
            weight, gradient, row_old, col_old, row_start, col_start = specs[index]
            lead = weight.shape[:-2]
            rows_here = section(3 * place).reshape((data_size, model_size) + lead + (weight.shape[-2],))
            cols_here = section(3 * place + 1).reshape((data_size, model_size) + lead + (weight.shape[-1],))
            weight_sum = jnp.sum(section(3 * place + 2), axis=(0, 1))
            if tall[index]:
                row_sum = jnp.moveaxis(jnp.sum(rows_here, axis=1), 0, -2).reshape(row_old.shape)
                col_sum = jnp.moveaxis(jnp.sum(cols_here, axis=0), 0, -2).reshape(col_old.shape)
            else:
                row_sum = jnp.moveaxis(jnp.swapaxes(rows_here, 0, 1), (0, 1), (-3, -2)).reshape(row_old.shape)
                col_sum = jnp.sum(cols_here, axis=(0, 1))
            row_new = decay_rate * row_old + (1.0 - decay_rate) * row_sum / col_old.shape[-1]
            col_new = decay_rate * col_old + (1.0 - decay_rate) * col_sum / row_old.shape[-1]
            row_mean = jnp.mean(row_new, axis=-1)[..., None, None]
            my_rows = lax.dynamic_slice_in_dim(row_new, row_start, weight.shape[-2], row_new.ndim - 1)
            my_cols = lax.dynamic_slice_in_dim(col_new, col_start, weight.shape[-1], col_new.ndim - 1)
            update = gradient * lax.rsqrt(my_rows[..., :, None] * my_cols[..., None, :] / row_mean)
            update_parts.append(jnp.sum(update * update, axis=(-2, -1)).reshape(-1))
            count_all = row_old.shape[-1] * col_old.shape[-1]
            pending.append(
                (weight, gradient, update, (row_new, col_new), weight_sum, count_all, lead + (1, 1))
            )
        if vectors_too:
            base = 3 * len(chosen)
            vector_sum = jnp.sum(section(base + 2), axis=(0, 1)).reshape(5, width)
            mine = lax.dynamic_slice_in_dim(vector_sum, data_index * gains.shape[1], gains.shape[1], 1)
            for weight, gradient, second_old, place in (
                (gains, mine[:2], second_gains, base),
                (router, mine[2:], second_router, base + 1),
            ):
                second_new = decay_rate * second_old + (1.0 - decay_rate) * (gradient * gradient + tiny_square)
                update = gradient * lax.rsqrt(second_new)
                update_parts.append(jnp.sum(update * update, axis=-1) / model_size)
                weight_sum = jnp.sum(section(place), axis=(0, 1))
                pending.append(
                    (weight, gradient, update, (second_new,), weight_sum, D, (weight.shape[0], 1))
                )
        update_pack = jnp.concatenate(update_parts)
        padding = -update_pack.shape[0] % 128
        update_sums = jnp.sum(all_parts(jnp.pad(update_pack, (0, padding))), axis=0)
        results = []
        at = 0
        for weight, gradient, update, moments, weight_sum, count_all, lead_shape in pending:
            lead_count = weight_sum.shape[0]
            update_sum = update_sums[at : at + lead_count]
            at = at + lead_count
            new_weight = scaled_step(weight, update, weight_sum, update_sum, count_all, lead_shape)
            results.append([gradient, *moments, new_weight])
        return results

    ffn_results = updated((2, 3, 4, 5), False)
    attn_results = updated((0, 1), True)
    results = [mixed, grad_tokens]
    for result in attn_results[:2] + ffn_results + attn_results[2:]:
        results.extend(result)
    return tuple(results)


def solution(mesh):
    placed = (
        P(None, "dp", None),
        P(None, "dp", None),
        P(),
        P(None, "dp"),
        P(),
        P(None, "dp"),
        P(None, "dp", "mp"),
        P(None, ("mp", "dp"), None),
        P(None, "dp", "mp"),
        P(("mp", "dp"), None),
        P(None, "dp", "mp"),
        P(("mp", "dp"), None),
        P(None, "dp"),
        P(None, "dp"),
        P(),
        P(),
        P(),
        P(),
        P(),
        P(),
        P(),
        P(),
        P(),
        P(),
        P(),
        P(),
        P(None, "dp"),
        P(None, "dp"),
    )
    return jax.shard_map(
        shards,
        mesh=mesh,
        in_specs=placed,
        out_specs=(
            P(None, "dp", None),
            P(None, "dp", None),
            P(None, "dp", "mp"),
            P(),
            P(),
            P(None, "dp", "mp"),
            P(None, ("mp", "dp"), None),
            P(),
            P(),
            P(None, ("mp", "dp"), None),
            P(None, "dp", "mp"),
            P(),
            P(),
            P(None, "dp", "mp"),
            P(("mp", "dp"), None),
            P(),
            P(),
            P(("mp", "dp"), None),
            P(None, "dp", "mp"),
            P(),
            P(),
            P(None, "dp", "mp"),
            P(("mp", "dp"), None),
            P(),
            P(),
            P(("mp", "dp"), None),
            P(None, "dp"),
            P(None, "dp"),
            P(None, "dp"),
            P(None, "dp"),
            P(None, "dp"),
            P(None, "dp"),
        ),
        check_vma=False,
    )
```

time: 1910 us -> 658 us (0.34)
  waiting for transfers between devices: 851 us -> 257 us
  blocking collectives: 291 us -> 0 us
  other arithmetic: 310 us -> 60.1 us
  Pallas kernels: 0 us -> 193 us
  matrix products: 172 us -> 2.62 us
  local copies, waits for them, and re-layouts: 220 us -> 57.3 us
  starting transfers between devices: 25.9 us -> 60.2 us
    unnamed x20 -> x4, waiting for transfers between devices: 444 us -> 0.07 us
    all_gather x7 -> x0, blocking collectives: 193 us -> none  [the longest x2 56.2 us: shards(): lax.all_gather(jnp.concatenate([heavy_key, scaled_value], axis=-1), 'dp',...]
    pallas_call x0 -> x15, Pallas kernels: none -> 193 us  [the longest x14 186 us: kernel_call(): pl.pallas_call(body, out_shape=outs, in_specs=[smem] * scalars + [vmem] *...]
    psum x4 -> x0, waiting for transfers between devices: 169 us -> none  [the longest x1 102 us: shards(): lax.psum((jnp.concatenate(row_parts), jnp.concatenate(col_parts), jnp.con...]
    dot_general x82 -> x1, matrix products: 167 us -> 2.62 us  [shards(): jnp.einsum('mrt,mtd->mrd', picks, tokens, preferred_element_type=wide)]
    reduce_scatter x5 -> x2, waiting for transfers between devices: 191 us -> 52 us  [the longest x1 52 us: shards(): lax.psum_scatter(pack_attn, 'dp', scatter_dimension=0, tiled=True)]
    ppermute x8 -> x31, waiting for transfers between devices: 0.02 us -> 122 us  [the longest x8 106 us: mp_sum(): near = lax.ppermute((mine + theirs).astype(low), 'mp', far_pairs)]
    psum x4 -> x0, blocking collectives: 97.3 us -> none  [the longest x1 42 us: shards(): update_sums = lax.psum(jnp.concatenate(update_parts), ('dp', 'mp'))]
  transfers between devices with their start and end apart: 24 -> 41, of which waited for: 13 -> 19; matrix products, arithmetic and copies ran while one was open for 22% -> 14% of each run, Pallas kernels for 0% -> 25%
where the time goes in v1:
time: 658 us; the launch traced here: 651 us
  waiting for transfers between devices  257 us (39%)
  Pallas kernels  193 us (29%)
  starting transfers between devices  60.2 us (9%)
  other arithmetic  60.1 us (9%)
  local copies, waits for them, and re-layouts  57.3 us (9%)
  between operations  20.2 us (3%)
    pallas_call x14, Pallas kernels, kernel_call(): pl.pallas_call(body, out_shape=outs, in_specs=[smem] * scalars + [vmem] *...  186 us
    ppermute x8, waiting for transfers between devices, mp_sum(): near = lax.ppermute((mine + theirs).astype(low), 'mp', far_pairs)  106 us
    all_gather x1, waiting for transfers between devices, shards(): got_one = lax.all_gather(pack_one, 'dp', axis=0, tiled=False)  60 us
    reduce_scatter x1, waiting for transfers between devices, shards(): lax.psum_scatter(pack_attn, 'dp', scatter_dimension=0, tiled=True)  52 us
    all_to_all x4, starting transfers between devices, all_parts(): return lax.all_to_all(sent, ('dp', 'mp'), 0, 0, tiled=True)  31.2 us
    all_to_all x4, waiting for transfers between devices, all_parts(): return lax.all_to_all(sent, ('dp', 'mp'), 0, 0, tiled=True)  15.3 us
  transfers between devices with their start and end apart: 41, of which 19 were waited for; matrix products, arithmetic and copies ran while one was open for 14% of the time, Pallas kernels for 25%

profile of v1, /device:TPU:0, one launch (start us, length us, event | category | flops | bytes accessed | tf_op | source)
XLA Modules:
  0.0 650.5 jit_solution(7068639935991785417)
XLA Ops:
  22.4 60.0 %all-gather.5.cloned.1.call-done = bf16[4224,384]{1,0:T(8,128)(2,1)} async-done(((bf16[528,384]{1,0:T(8,128)(2,1)}), bf16[4224,384]{1,0:T(8,128)(2,1)}) %all-gather.5.cloned.1.call-update) | async-done | bytes 3244048 | tf_op jit(solution)/shard_map/all_gather | solution.py:802
  94.9 11.5 %shard_map.516 = (bf16[2,1024,768]{2,1,0:T(8,128)(2,1)}, bf16[2,1024,192]{2,1,0:T(8,128)(2,1)}, bf16[2,1024,192]{2,1,0:T(8,128)(2,1)}, bf16[2,1024,192]{2,1,0:T(...) custom-call(bf16[2,1024,768]{2,1,0:T(8,128)(2,1)} %refs_10_.1, ...), custom_call_target="tpu_custom_call" | custom-call | flops 5000000000 | bytes 12512256 | tf_op jit(solution)/shard_map/pallas_call | solution.py:106
  135.3 11.0 %shard_map.518 = (bf16[1024,768]{1,0:T(8,128)(2,1)}, bf16[1024,192]{1,0:T(8,128)(2,1)}, bf16[128,192]{1,0:T(8,128)(2,1)}, f32[128,768]{1,0:T(8,128)}) custom-call(bf16[1024,192]{1,0:T(8,128)(2,1)} %get-tuple-element.445.q_ref, bf16[1024,192]{1,0:T(8,128)(2,1)} %get-tuple-element.508.k_ref, bf16[1024,192]{1,0:T(8,128)(2,1)} %get-tuple-element.441.v_ref, ...), custom_call_target="tpu_custom_call" | custom-call | flops 4000000000 | bytes 5126144 | tf_op jit(solution)/shard_map/pallas_call | solution.py:106
  148.2 11.2 %shard_map.520 = (bf16[1024,768]{1,0:T(8,128)(2,1)}, bf16[1024,192]{1,0:T(8,128)(2,1)}, bf16[128,192]{1,0:T(8,128)(2,1)}, f32[128,768]{1,0:T(8,128)}) custom-call(bf16[1024,192]{1,0:T(8,128)(2,1)} %get-tuple-element.444.q_ref, bf16[1024,192]{1,0:T(8,128)(2,1)} %get-tuple-element.509.k_ref, bf16[1024,192]{1,0:T(8,128)(2,1)} %get-tuple-element.440.v_ref, ...), custom_call_target="tpu_custom_call" | custom-call | flops 4000000000 | bytes 5126144 | tf_op jit(solution)/shard_map/pallas_call | solution.py:106
  165.1 17.0 %collective-permute-done.6.near_ref = bf16[512,768]{1,0:T(8,128)(2,1)} collective-permute-done((bf16[512,768]{1,0:T(8,128)(2,1)S(1)}, bf16[512,768]{1,0:T(8,128)(2,1)}, u32[]{:S(2)}, u32[]{:S(2)}) %collective-permute-start.6) | collective-permute-done | bytes 786464 | tf_op jit(solution)/shard_map/ppermute | solution.py:954
  184.8 13.2 %collective-permute-done.9.near_ref = bf16[512,768]{1,0:T(8,128)(2,1)} collective-permute-done((bf16[512,768]{1,0:T(8,128)(2,1)S(1)}, bf16[512,768]{1,0:T(8,128)(2,1)}, u32[]{:S(2)}, u32[]{:S(2)}) %collective-permute-start.9) | collective-permute-done | bytes 786464 | tf_op jit(solution)/shard_map/ppermute | solution.py:954
  200.1 19.8 %shard_map.519 = (f32[1024,768]{1,0:T(8,128)}, bf16[1024,768]{1,0:T(8,128)(2,1)}, bf16[1024,768]{1,0:T(8,128)(2,1)}, bf16[1024,768]{1,0:T(8,128)(2,1)}, bf16[102...) custom-call(s32[1]{0:T(128)} %bitcast.core_ref, ...), custom_call_target="tpu_custom_call" | custom-call | flops 6000000000 | bytes 24408068 | tf_op jit(solution)/shard_map/pallas_call | solution.py:106
  220.8 20.2 %shard_map.521 = (f32[1024,768]{1,0:T(8,128)}, bf16[1024,768]{1,0:T(8,128)(2,1)}, bf16[1024,768]{1,0:T(8,128)(2,1)}, bf16[1024,768]{1,0:T(8,128)(2,1)}, bf16[102...) custom-call(s32[1]{0:T(128)} %bitcast.core_ref, ...), custom_call_target="tpu_custom_call" | custom-call | flops 6000000000 | bytes 24408068 | tf_op jit(solution)/shard_map/pallas_call | solution.py:106
  241.0 12.0 %shard_map.529 = bf16[8,1440,256]{2,1,0:T(8,128)(2,1)} custom-call(bf16[2,1024,768]{2,1,0:T(8,128)(2,1)} %cot_ref.1, bf16[1024,768]{1,0:T(8,128)(2,1)} %get-tuple-element.176.refs_0_, bf16[1024,256]{1,0:T(8,128)(2,1)} %get-tuple-element.177.refs_1_, bf16[2,1024,256]{2,1,0:T(8,128)(2,1)} %get-tuple-element.178.refs_2_, ...), custom_call_target="tpu_custom_call" | custom-call | flops 4000000000 | bytes 17694720 | tf_op jit(solution)/shard_map/pallas_call | solution.py:106
  264.4 16.5 %collective-permute-done.12.near_ref = bf16[512,768]{1,0:T(8,128)(2,1)} collective-permute-done((bf16[512,768]{1,0:T(8,128)(2,1)S(1)}, bf16[512,768]{1,0:T(8,128)(2,1)}, u32[]{:S(2)}, u32[]{:S(2)}) %collective-permute-start.12) | collective-permute-done | bytes 786464 | tf_op jit(solution)/shard_map/ppermute | solution.py:954
  282.7 14.5 %collective-permute-done.20.near_ref = bf16[512,768]{1,0:T(8,128)(2,1)} collective-permute-done((bf16[512,768]{1,0:T(8,128)(2,1)S(1)}, bf16[512,768]{1,0:T(8,128)(2,1)}, u32[]{:S(2)}, u32[]{:S(2)}) %collective-permute-start.20) | collective-permute-done | bytes 786464 | tf_op jit(solution)/shard_map/ppermute | solution.py:954
  298.0 21.9 %shard_map.524 = (f32[1024,768]{1,0:T(8,128)}, bf16[1024,768]{1,0:T(8,128)(2,1)}, f32[1,768]{1,0:T(1,128)}, bf16[1024,192]{1,0:T(8,128)(2,1)}, f32[2,1024,192]{2...) custom-call(s32[1]{0:T(128)} %bitcast.core_ref, ...), custom_call_target="tpu_custom_call" | custom-call | flops 8000000000 | bytes 20788740 | tf_op jit(solution)/shard_map/pallas_call | solution.py:106
  327.9 21.7 %shard_map.523 = (f32[1024,768]{1,0:T(8,128)}, bf16[1024,768]{1,0:T(8,128)(2,1)}, f32[1,768]{1,0:T(1,128)}, bf16[1024,192]{1,0:T(8,128)(2,1)}, f32[2,1024,192]{2...) custom-call(s32[1]{0:T(128)} %bitcast.core_ref, ...), custom_call_target="tpu_custom_call" | custom-call | flops 8000000000 | bytes 20788740 | tf_op jit(solution)/shard_map/pallas_call | solution.py:106
  378.8 7.6 %shard_map.526 = (bf16[1024,768]{1,0:T(8,128)(2,1)}, bf16[2,1024,192]{2,1,0:T(8,128)(2,1)}, f32[2,768]{1,0:T(2,128)}) custom-call(bf16[1024,192]{1,0:T(8,128)(2,1)} %get-tuple-element.151.dq_ref.refs_9_, f32[2,1024,192]{2,1,0:T(8,128)} %get-tuple-element.152.inner_ref, bf16[2,64,192]{2,1,0:T(8,128)(2,1)} %get-tuple-element.466.prev_ref, ...), custom_call_target="tpu_custom_call" | custom-call | flops 3000000000 | bytes 7847424 | tf_op jit(solution)/shard_map/pallas_call | solution.py:106
  388.9 7.5 %shard_map.525 = (bf16[1024,768]{1,0:T(8,128)(2,1)}, bf16[2,1024,192]{2,1,0:T(8,128)(2,1)}, f32[2,768]{1,0:T(2,128)}) custom-call(bf16[1024,192]{1,0:T(8,128)(2,1)} %get-tuple-element.139.dq_ref.refs_0_, f32[2,1024,192]{2,1,0:T(8,128)} %get-tuple-element.140.inner_ref, bf16[2,64,192]{2,1,0:T(8,128)(2,1)} %get-tuple-element.467.prev_ref, ...), custom_call_target="tpu_custom_call" | custom-call | flops 3000000000 | bytes 7847424 | tf_op jit(solution)/shard_map/pallas_call | solution.py:106
  406.6 12.2 %collective-permute-done.29.refs_6_ = bf16[512,768]{1,0:T(8,128)(2,1)} collective-permute-done((bf16[512,768]{1,0:T(8,128)(2,1)S(1)}, bf16[512,768]{1,0:T(8,128)(2,1)}, u32[]{:S(2)}, u32[]{:S(2)}) %collective-permute-start.29) | collective-permute-done | bytes 786464 | tf_op jit(solution)/shard_map/ppermute | solution.py:954
  418.8 16.8 %collective-permute-done.26.refs_2_ = bf16[512,768]{1,0:T(8,128)(2,1)} collective-permute-done((bf16[512,768]{1,0:T(8,128)(2,1)}, bf16[512,768]{1,0:T(8,128)(2,1)}, u32[]{:S(2)}, u32[]{:S(2)}) %collective-permute-start.26) | collective-permute-done | bytes 786464 | tf_op jit(solution)/shard_map/ppermute | solution.py:954
  435.7 15.9 %collective-permute-done.17.refs_8_ = bf16[512,768]{1,0:T(8,128)(2,1)S(1)} collective-permute-done((bf16[512,768]{1,0:T(8,128)(2,1)}, bf16[512,768]{1,0:T(8,128)(2,1)S(1)}, u32[]{:S(2)}, u32[]{:S(2)}) %collective-permute-start.17) | collective-permute-done | bytes 786464 | tf_op jit(solution)/shard_map/ppermute | solution.py:954
  459.6 17.8 %all-to-all-start.4 = ((f32[32,1,5120]{2,1,0:T(1,128)}), f32[32,1,5120]{2,1,0:T(1,128)S(1)}, u32[]{:S(2)}, u32[]{:S(2)}) async-start(f32[32,1,5120]{2,1,0:T(1,128)} %broadcast_in_dim.65), calls=%async_computation.6 | async-start | bytes 1310720 | tf_op jit(solution)/shard_map/all_to_all | solution.py:1211
  477.5 12.5 %shard_map.528 = bf16[8,384,384]{2,1,0:T(8,128)(2,1)} custom-call(bf16[2,1024,768]{2,1,0:T(8,128)(2,1)} %get-tuple-element.161.normed_ref, bf16[2,128,768]{2,1,0:T(8,128)(2,1)} %get-tuple-element.162.query_ref, bf16[2,1024,768]{2,1,0:T(8,128)(2,1)} %bitcast.259, bf16[1024,192]{1,0:T(8,128)(2,1)} %get-tuple-element.139.dq_ref.refs_0_, ...), custom_call_target="tpu_custom_call" | custom-call | flops 4000000000 | bytes 17498112 | tf_op jit(solution)/shard_map/pallas_call | solution.py:106
  490.0 14.6 %shard_map.527 = (f32[2,1024,768]{2,1,0:T(8,128)}, f32[1,768]{1,0:T(1,128)}) custom-call(s32[1]{0:T(128)} %bitcast.core_ref, bf16[1024,768]{1,0:T(8,128)(2,1)} %get-tuple-element.150.refs_0_, bf16[1024,768]{1,0:T(8,128)(2,1)} %copy-done.4, bf16[512,768]{1,0:T(8,128)(2,1)} %collective-permute-done.26.refs_2_, ...), custom_call_target="tpu_custom_call" | custom-call | bytes 25193476 | tf_op jit(solution)/shard_map/pallas_call | solution.py:106
  505.4 9.6 %shard_map.522 = bf16[2,1024,768]{2,1,0:T(8,128)(2,1)} custom-call(s32[1]{0:T(128)} %bitcast.core_ref, f32[1024,768]{1,0:T(8,128)} %get-tuple-element.128.refs_0_.middle_ref, bf16[1024,768]{1,0:T(8,128)(2,1)} %get-tuple-element.132.refs_1_, bf16[1024,768]{1,0:T(8,128)(2,1)} %copy-done.7, bf16[512,768]{1,0:T(8,128)(2,1)} %collective-permute-done.14.refs_3_, ...), custom_call_target="tpu_custom_call" | custom-call | bytes 18874372 | tf_op jit(solution)/shard_map/pallas_call | solution.py:106
  535.3 52.0 %reduce-scatter.5.cloned.1.call-done = bf16[384,384]{1,0:T(8,128)(2,1)} async-done(((bf16[3072,384]{1,0:T(8,128)(2,1)}), bf16[384,384]{1,0:T(8,128)(2,1)}) %reduce-scatter.5.cloned.1.call-update) | async-done | bytes 294928 | tf_op jit(solution)/shard_map/reduce_scatter | solution.py:1158
  611.7 8.3 %all-to-all-done.2 = f32[32,1,7168]{2,1,0:T(1,128)S(1)} async-done(((f32[32,1,7168]{2,1,0:T(1,128)}), f32[32,1,7168]{2,1,0:T(1,128)S(1)}, u32[]{:S(2)}, u32[]{:S(2)}) %all-to-all-start.2) | async-done | bytes 917536 | tf_op jit(solution)/shard_map/all_to_all | solution.py:1211
  (540 shorter events, 205.1 us)
Async XLA Ops:
  7.2 75.1 %all-gather.5.cloned.1.call-start = ((), (), s32[]{:S(2)}) async-start(), calls=%async_computation.10 | async-start | bytes 3649536 | tf_op jit(solution)/shard_map/all_gather | solution.py:802
  17.9 182.2 %all-gather.7.cloned.1.call-start = ((), (), s32[]{:S(2)}) async-start(), calls=%async_computation.11 | async-start | bytes 6635520 | tf_op jit(solution)/shard_map/all_gather | solution.py:854
  82.4 369.2 %reduce-scatter.3.cloned.1.call-start = ((), (), s32[]{:S(2)}) async-start(), calls=%async_computation.8 | async-start | bytes 6635520 | tf_op jit(solution)/shard_map/reduce_scatter | solution.py:1046
  94.9 28.8 %collective-permute-start.2 = (bf16[8,2,32,768]{3,2,1,0:T(8,128)(2,1)}, bf16[8,2,32,768]{3,2,1,0:T(8,128)(2,1)S(1)}, u32[]{:S(2)}, u32[]{:S(2)}) collective-permute-start(bf16[8,2,32,768]{3,2,1,0:T(8,128)(2,1)} %get-tuple-element.121.o_ref), channel_id=1, source_target_pairs={{0,1},{1,0},{2,3},{3,2},{4,5},{5,4},{6,7},{7,6},{8,9},{9,8},{10,11... | collective-permute-start | bytes 2359304 | tf_op jit(solution)/shard_map/ppermute | solution.py:915
  161.6 20.6 %collective-permute-start.6 = (bf16[512,768]{1,0:T(8,128)(2,1)S(1)}, bf16[512,768]{1,0:T(8,128)(2,1)}, u32[]{:S(2)}, u32[]{:S(2)}) collective-permute-start(bf16[512,768]{1,0:T(8,128)(2,1)S(1)} %add_convert_fusion.7), channel_id=1, source_target_pairs={{0,2},{1,3},{2,0},{3,1},{4,6},{5,7},{6,4},{7,5},{8,10},{9,11},{10,... | collective-permute-start | bytes 2359304 | tf_op jit(solution)/shard_map/ppermute | solution.py:954
  164.6 33.5 %collective-permute-start.9 = (bf16[512,768]{1,0:T(8,128)(2,1)S(1)}, bf16[512,768]{1,0:T(8,128)(2,1)}, u32[]{:S(2)}, u32[]{:S(2)}) collective-permute-start(bf16[512,768]{1,0:T(8,128)(2,1)S(1)} %add_convert_fusion.6), channel_id=1, source_target_pairs={{0,2},{1,3},{2,0},{3,1},{4,6},{5,7},{6,4},{7,5},{8,10},{9,11},{10,... | collective-permute-start | bytes 2359304 | tf_op jit(solution)/shard_map/ppermute | solution.py:954
  198.1 21.8 %collective-permute-start.10 = (bf16[512,768]{1,0:T(8,128)(2,1)}, bf16[512,768]{1,0:T(8,128)(2,1)S(1)}, u32[]{:S(2)}, u32[]{:S(2)}) collective-permute-start(bf16[512,768]{1,0:T(8,128)(2,1)} %collective-permute-done.9.near_ref), channel_id=1, source_target_pairs={{0,1},{1,0},{2,3},{3,2},{4,5},{5,4},{6,7},{7,6},{8,9},{9,8},{10,11... | collective-permute-start | bytes 2359304 | tf_op jit(solution)/shard_map/ppermute | solution.py:955
  260.3 20.5 %collective-permute-start.12 = (bf16[512,768]{1,0:T(8,128)(2,1)S(1)}, bf16[512,768]{1,0:T(8,128)(2,1)}, u32[]{:S(2)}, u32[]{:S(2)}) collective-permute-start(bf16[512,768]{1,0:T(8,128)(2,1)S(1)} %add_convert_fusion.5), channel_id=1, source_target_pairs={{0,2},{1,3},{2,0},{3,1},{4,6},{5,7},{6,4},{7,5},{8,10},{9,11},{10,... | collective-permute-start | bytes 2359304 | tf_op jit(solution)/shard_map/ppermute | solution.py:954
  262.9 34.3 %collective-permute-start.20 = (bf16[512,768]{1,0:T(8,128)(2,1)S(1)}, bf16[512,768]{1,0:T(8,128)(2,1)}, u32[]{:S(2)}, u32[]{:S(2)}) collective-permute-start(bf16[512,768]{1,0:T(8,128)(2,1)S(1)} %add_convert_fusion.2), channel_id=1, source_target_pairs={{0,2},{1,3},{2,0},{3,1},{4,6},{5,7},{6,4},{7,5},{8,10},{9,11},{10,... | collective-permute-start | bytes 2359304 | tf_op jit(solution)/shard_map/ppermute | solution.py:954
  297.2 30.8 %collective-permute-start.21 = (bf16[512,768]{1,0:T(8,128)(2,1)}, bf16[512,768]{1,0:T(8,128)(2,1)}, u32[]{:S(2)}, u32[]{:S(2)}) collective-permute-start(bf16[512,768]{1,0:T(8,128)(2,1)} %collective-permute-done.20.near_ref), channel_id=1, source_target_pairs={{0,1},{1,0},{2,3},{3,2},{4,5},{5,4},{6,7},{7,6},{8,9},{9,8},{10,11... | collective-permute-start | bytes 2359304 | tf_op jit(solution)/shard_map/ppermute | solution.py:955
  322.5 35.0 %all-to-all-start.1 = ((bf16[8,128,384]{2,1,0:T(8,128)(2,1)}), bf16[8,128,384]{2,1,0:T(8,128)(2,1)}, u32[]{:S(2)}, u32[]{:S(2)}) async-start(bf16[8,128,384]{2,1,0:T(8,128)(2,1)} %bitcast.75), calls=%async_computation.1 | async-start | bytes 1572864 | tf_op jit(solution)/shard_map/all_to_all | solution.py:1092
  327.6 48.3 %collective-permute-start.13 = (bf16[1024,768]{1,0:T(8,128)(2,1)S(1)}, bf16[1024,768]{1,0:T(8,128)(2,1)S(1)}, u32[]{:S(2)}, u32[]{:S(2)}) collective-permute-start(bf16[1024,768]{1,0:T(8,128)(2,1)S(1)} %copy-done.5), channel_id=1, source_target_pairs={{0,1},{1,0},{2,3},{3,2},{4,5},{5,4},{6,7},{7,6},{8,9},{9,8},{10,11... | collective-permute-start | bytes 4718600 | tf_op jit(solution)/shard_map/ppermute | solution.py:951
  357.5 31.4 %all-to-all-start = ((bf16[8,128,384]{2,1,0:T(8,128)(2,1)}), bf16[8,128,384]{2,1,0:T(8,128)(2,1)}, u32[]{:S(2)}, u32[]{:S(2)}) async-start(bf16[8,128,384]{2,1,0:T(8,128)(2,1)} %bitcast.260), calls=%async_computation | async-start | bytes 1572864 | tf_op jit(solution)/shard_map/all_to_all | solution.py:1092
  398.2 20.6 %collective-permute-start.29 = (bf16[512,768]{1,0:T(8,128)(2,1)S(1)}, bf16[512,768]{1,0:T(8,128)(2,1)}, u32[]{:S(2)}, u32[]{:S(2)}) collective-permute-start(bf16[512,768]{1,0:T(8,128)(2,1)S(1)} %add_convert_fusion), channel_id=1, source_target_pairs={{0,2},{1,3},{2,0},{3,1},{4,6},{5,7},{6,4},{7,5},{8,10},{9,11},{10,... | collective-permute-start | bytes 2359304 | tf_op jit(solution)/shard_map/ppermute | solution.py:954
  401.3 34.4 %collective-permute-start.26 = (bf16[512,768]{1,0:T(8,128)(2,1)}, bf16[512,768]{1,0:T(8,128)(2,1)}, u32[]{:S(2)}, u32[]{:S(2)}) collective-permute-start(bf16[512,768]{1,0:T(8,128)(2,1)} %add_convert_fusion.1), channel_id=1, source_target_pairs={{0,2},{1,3},{2,0},{3,1},{4,6},{5,7},{6,4},{7,5},{8,10},{9,11},{10,... | collective-permute-start | bytes 2359304 | tf_op jit(solution)/shard_map/ppermute | solution.py:954
  403.7 47.9 %collective-permute-start.17 = (bf16[512,768]{1,0:T(8,128)(2,1)}, bf16[512,768]{1,0:T(8,128)(2,1)S(1)}, u32[]{:S(2)}, u32[]{:S(2)}) collective-permute-start(bf16[512,768]{1,0:T(8,128)(2,1)} %add_convert_fusion.3), channel_id=1, source_target_pairs={{0,2},{1,3},{2,0},{3,1},{4,6},{5,7},{6,4},{7,5},{8,10},{9,11},{10,... | collective-permute-start | bytes 2359304 | tf_op jit(solution)/shard_map/ppermute | solution.py:954
  406.5 98.8 %collective-permute-start.15 = (bf16[512,768]{1,0:T(8,128)(2,1)}, bf16[512,768]{1,0:T(8,128)(2,1)}, u32[]{:S(2)}, u32[]{:S(2)}) collective-permute-start(bf16[512,768]{1,0:T(8,128)(2,1)} %collective-permute-done.14.refs_3_), channel_id=1, source_target_pairs={{0,1},{1,0},{2,3},{3,2},{4,5},{5,4},{6,7},{7,6},{8,9},{9,8},{10,11... | collective-permute-start | bytes 2359304 | tf_op jit(solution)/shard_map/ppermute | solution.py:955
  418.8 71.2 %collective-permute-start.30 = (bf16[512,768]{1,0:T(8,128)(2,1)}, bf16[512,768]{1,0:T(8,128)(2,1)}, u32[]{:S(2)}, u32[]{:S(2)}) collective-permute-start(bf16[512,768]{1,0:T(8,128)(2,1)} %collective-permute-done.29.refs_6_), channel_id=1, source_target_pairs={{0,1},{1,0},{2,3},{3,2},{4,5},{5,4},{6,7},{7,6},{8,9},{9,8},{10,11... | collective-permute-start | bytes 2359304 | tf_op jit(solution)/shard_map/ppermute | solution.py:955
  435.7 54.3 %collective-permute-start.27 = (bf16[512,768]{1,0:T(8,128)(2,1)}, bf16[512,768]{1,0:T(8,128)(2,1)}, u32[]{:S(2)}, u32[]{:S(2)}) collective-permute-start(bf16[512,768]{1,0:T(8,128)(2,1)} %collective-permute-done.26.refs_2_), channel_id=1, source_target_pairs={{0,1},{1,0},{2,3},{3,2},{4,5},{5,4},{6,7},{7,6},{8,9},{9,8},{10,11... | collective-permute-start | bytes 2359304 | tf_op jit(solution)/shard_map/ppermute | solution.py:955
  451.5 53.8 %collective-permute-start.18 = (bf16[512,768]{1,0:T(8,128)(2,1)S(1)}, bf16[512,768]{1,0:T(8,128)(2,1)}, u32[]{:S(2)}, u32[]{:S(2)}) collective-permute-start(bf16[512,768]{1,0:T(8,128)(2,1)S(1)} %collective-permute-done.17.refs_8_), channel_id=1, source_target_pairs={{0,1},{1,0},{2,3},{3,2},{4,5},{5,4},{6,7},{7,6},{8,9},{9,8},{10,11... | collective-permute-start | bytes 2359304 | tf_op jit(solution)/shard_map/ppermute | solution.py:955
  459.6 57.3 %all-to-all-start.4 = ((f32[32,1,5120]{2,1,0:T(1,128)}), f32[32,1,5120]{2,1,0:T(1,128)S(1)}, u32[]{:S(2)}, u32[]{:S(2)}) async-start(f32[32,1,5120]{2,1,0:T(1,128)} %broadcast_in_dim.65), calls=%async_computation.6 | async-start | bytes 1310720 | tf_op jit(solution)/shard_map/all_to_all | solution.py:1211
  477.4 109.9 %reduce-scatter.5.cloned.1.call-start = ((), (), s32[]{:S(2)}) async-start(), calls=%async_computation.9 | async-start | bytes 2654208 | tf_op jit(solution)/shard_map/reduce_scatter | solution.py:1158
  529.5 61.8 %all-to-all-start.5 = ((f32[32,1,128]{2,1,0:T(1,128)}), f32[32,1,128]{2,1,0:T(1,128)S(1)}, u32[]{:S(2)}, u32[]{:S(2)}) async-start(f32[32,1,128]{2,1,0:T(1,128)} %broadcast_in_dim.110), calls=%async_computation.7 | async-start | bytes 32768 | tf_op jit(solution)/shard_map/all_to_all | solution.py:1211
  592.7 27.3 %all-to-all-start.2 = ((f32[32,1,7168]{2,1,0:T(1,128)}), f32[32,1,7168]{2,1,0:T(1,128)S(1)}, u32[]{:S(2)}, u32[]{:S(2)}) async-start(f32[32,1,7168]{2,1,0:T(1,128)} %broadcast_in_dim.63), calls=%async_computation.4 | async-start | bytes 1835008 | tf_op jit(solution)/shard_map/all_to_all | solution.py:1211
  (119 other events, 2147.4 us)
Sparse Core Ops, SparseCore 0:
  18.0 64.2 all-gather.4
  84.5 95.6 all-gather.6
  253.1 130.3 reduce-scatter.2
  517.0 70.3 reduce-scatter.4
